TPU v7x, 32 devices: a whole 2x2x4 slice. The times are simulated.
32 devices in a mesh: ep: 16 (over z, x, core), tp: 2 (over y).
Axes of the slice: x: 2, y: 2, z: 4, core: 2. Of those that a mesh axis runs over, the one named last changes fastest.
Arguments:
- residual_in: bfloat16 [3072, 2048], P('ep'), may hold values from -6 to 6
- shortcut: bfloat16 [3072, 2048], P('ep'), may hold values from -6 to 6
- attn_gain: float32 [2048], replicated, may hold values from 0.25 to 1.75
- moe_gain: float32 [2048], replicated, may hold values from 0.25 to 1.75
- query_weight: bfloat16 [2048, 4096], P('ep', 'tp')
- key_value: bfloat16 [2048, 1024], P('ep')
- output_weight: bfloat16 [2048, 4096], P('ep', 'tp'), may hold values from -0.09375 to 0.09375
- query_gain: float32 [128], replicated, may hold values from 0.5 to 5
- key_gain: float32 [128], replicated, may hold values from 0.5 to 5
- router_weight: bfloat16 [16, 2048], replicated, may hold values from -0.125 to 0.125
- expert_ids: int32 [3072, 8], P('ep'), may hold values from 0 to 15, all different within a row; in each aligned block of 192 rows (0 to 191, 192 to 383, ...) at most 120 rows name the same one
- gate_up_weight: bfloat16 [32, 2048, 1536], P(('ep', 'tp')), may hold values from -0.125 to 0.125
- down_weight: bfloat16 [32, 768, 2048], P(('ep', 'tp')), may hold values from -0.15625 to 0.15625
Outputs:
- layer_out: bfloat16 [3072, 2048], P('ep')
Inputs may be any that keep to these rules, and one draw needn't show every extreme that they name: `expert_ids`: each row names 8 different experts. Among the 192 rows of one sequence no expert is named by more than 120 rows, a bound that some block reaches.
All inputs are finite; a program needn't handle non-finite values.
Results may differ from a plain program's by a relative error of at most 0.009.
Values may be sent and summed in bfloat16 or wider, within the bound.
A program may use at most 128 MiB of HBM per device.

v0:
```python
import jax
import jax.numpy as jnp
from jax import lax
from jax.sharding import PartitionSpec as P

HD = 128
QH = 32
KVH = 4
TOPK = 8


EPS = 1e-06
ROPE_BASE = 1000000.0


def from_partner(value, axis, apart):
    mask = 2**apart
    pairs = [(source, source ^ mask) for source in range(lax.axis_size(axis))]
    return lax.ppermute(value, axis, pairs)


def norm_rows(values, gain):
    wide = values.astype(jnp.float32)
    return wide * lax.rsqrt(jnp.mean(wide * wide, -1, keepdims=True) + EPS) * gain


def rotary(values):
    length = values.shape[0]
    half = values.shape[-1] // 2
    position = jnp.arange(length, dtype=jnp.float32)
    freq = ROPE_BASE ** (-jnp.arange(half, dtype=jnp.float32) * 2.0 / values.shape[-1])
    angle = position[:, None] * freq[None, :]
    cosine = jnp.cos(angle)[:, None, :]
    sine = jnp.sin(angle)[:, None, :]
    first = values[..., :half]
    second = values[..., half:]
    return jnp.concatenate([first * cosine - second * sine, second * cosine + first * sine], -1)


def capacity_of(rows, experts):
    return max(2, 5 * rows * TOPK // (4 * experts))


def attend(query, keyval, query_gain, key_gain, kv_count):
    seq = query.shape[0]
    query = rotary(norm_rows(query.reshape(seq, -1, HD), query_gain)).astype(jnp.bfloat16)
    heads = query.shape[1]
    query = query.reshape(seq, kv_count, heads // kv_count, HD)
    keyval = keyval.reshape(seq, 2, kv_count, HD)
    keys = rotary(norm_rows(keyval[:, 0], key_gain)).astype(jnp.bfloat16)
    values = keyval[:, 1].astype(jnp.bfloat16)
    logits = jnp.einsum("sgjd,tgd->gjst", query, keys, preferred_element_type=jnp.float32) * HD ** (
        -0.5
    )
    causal = jnp.arange(seq)[:, None] >= jnp.arange(seq)[None, :]
    logits = jnp.where(causal, logits, -1e30)
    peak = jnp.max(logits, -1, keepdims=True)
    expo = jnp.exp(logits - peak)
    probs = (expo / jnp.sum(expo, -1, keepdims=True)).astype(jnp.bfloat16)
    attended = jnp.einsum("gjst,tgd->sgjd", probs, values, preferred_element_type=jnp.float32)
    return attended.astype(jnp.bfloat16).reshape(seq, heads * HD)


def project_out(attended, weight):
    return lax.dot_general(
        attended, weight, (((1,), (1,)), ((), ())), preferred_element_type=jnp.float32
    )


def local(
    residual_in,
    shortcut,
    attn_gain,
    moe_gain,
    query_weight,
    key_value,
    output_weight,
    query_gain,
    key_gain,
    router_weight,
    expert_ids,
    gate_up_weight,
    down_weight,
):
    n_ep = lax.axis_size("ep")
    n_tp = lax.axis_size("tp")
    rank = lax.axis_index("tp")
    pairs = n_tp // 2
    group_id = rank // 2
    side = rank % 2
    rows, d_model = residual_in.shape
    half_width = d_model // 2
    experts = router_weight.shape[0]
    capacity = capacity_of(rows, experts)
    ff_dev = down_weight.shape[1]
    qh_dev = query_weight.shape[1] // HD
    group = QH // KVH
    kv_count = max(1, qh_dev // group)
    kv_start = rank * qh_dev // group
    attn_rows = norm_rows(residual_in, attn_gain).astype(jnp.bfloat16)
    moe_rows = norm_rows(shortcut, moe_gain).astype(jnp.bfloat16)
    logits_router = lax.dot_general(
        moe_rows, router_weight, (((1,), (1,)), ((), ())), preferred_element_type=jnp.float32
    )
    hits = (expert_ids[:, :, None] == jnp.arange(experts, dtype=jnp.int32)[None, None, :]).astype(
        jnp.float32
    )
    chosen = jnp.sum(hits * logits_router[:, None, :], -1)
    scores = jax.nn.sigmoid(chosen)
    gates = (scores / jnp.sum(scores, 1, keepdims=True)).astype(jnp.bfloat16)
    per_row = jnp.sum(hits, 1).astype(jnp.bfloat16)
    lower = (jnp.arange(rows)[:, None] > jnp.arange(rows)[None, :]).astype(jnp.bfloat16)
    earlier = jnp.dot(lower, per_row, preferred_element_type=jnp.float32)
    slot = jnp.sum(hits * earlier[:, None, :], -1)
    mine = expert_ids % pairs == group_id
    target = (expert_ids // pairs).astype(jnp.float32) * capacity + slot
    target = jnp.where(mine, target, -1.0)
    places = jnp.arange(n_ep * capacity, dtype=jnp.float32)
    match = (target[:, :, None] == places[None, None, :]).astype(jnp.float32)
    dispatch_map = jnp.sum(match, 1).astype(jnp.bfloat16)
    combine = jnp.sum(match * gates.astype(jnp.float32)[:, :, None], 1).astype(jnp.bfloat16)
    outgoing = lax.dot_general(
        dispatch_map, moe_rows, (((0,), (0,)), ((), ())), preferred_element_type=jnp.float32
    ).astype(jnp.bfloat16)
    outgoing = outgoing.reshape(n_ep, capacity, d_model)
    arrived = lax.all_to_all(outgoing, "ep", split_axis=0, concat_axis=0, tiled=True)
    paired = jnp.einsum(
        "ack,kf->acf", arrived, gate_up_weight[0], preferred_element_type=jnp.float32
    )
    hidden = (jax.nn.silu(paired[..., :ff_dev]) * paired[..., ff_dev:]).astype(jnp.bfloat16)
    partial_sum = jnp.einsum(
        "acf,fk->ack", hidden, down_weight[0], preferred_element_type=jnp.float32
    )
    kept = lax.dynamic_slice_in_dim(partial_sum, side * half_width, half_width, 2)
    handed = lax.dynamic_slice_in_dim(partial_sum, (1 - side) * half_width, half_width, 2)
    received = from_partner(handed.astype(jnp.bfloat16), "tp", 0).astype(handed.dtype)
    expert_out = (kept + received).astype(jnp.bfloat16)
    returned = lax.all_to_all(expert_out, "ep", split_axis=0, concat_axis=0, tiled=True).reshape(
        -1, half_width
    )
    moe_cols = jnp.dot(combine, returned, preferred_element_type=jnp.float32)
    blank = jnp.zeros_like(moe_cols)
    moe_full = jnp.where(
        side == 0, jnp.concatenate([moe_cols, blank], 1), jnp.concatenate([blank, moe_cols], 1)
    )
    local_rows = key_value.shape[0]
    local_kv = lax.dynamic_slice_in_dim(
        key_value.reshape(local_rows, 2, KVH, HD), kv_start, kv_count, 2
    )
    local_kv = local_kv.reshape(local_rows, 2 * kv_count * HD)
    full_query, full_kv, full_out = (
        lax.all_gather(query_weight, "ep", axis=0, tiled=True),
        lax.all_gather(local_kv, "ep", axis=0, tiled=True),
        lax.all_gather(output_weight, "ep", axis=0, tiled=True),
    )
    query = jnp.dot(attn_rows, full_query, preferred_element_type=jnp.float32)
    keyval = jnp.dot(attn_rows, full_kv, preferred_element_type=jnp.float32)
    attended = attend(query, keyval, query_gain, key_gain, kv_count)
    attn_terms = project_out(attended, full_out)
    attn_part = attn_terms.astype(jnp.bfloat16).astype(jnp.float32)
    total = attn_part + moe_full
    summed = lax.psum(total, "tp")
    return (residual_in.astype(jnp.float32) + summed).astype(jnp.bfloat16)


def solution(mesh):
    return jax.shard_map(
        local,
        mesh=mesh,
        in_specs=(
            P("ep", None),
            P("ep", None),
            P(),
            P(),
            P("ep", "tp"),
            P("ep", None),
            P("ep", "tp"),
            P(),
            P(),
            P(),
            P("ep", None),
            P(("ep", "tp"), None, None),
            P(("ep", "tp"), None, None),
        ),
        out_specs=P("ep", None),
        check_vma=False,
    )
```

profile of v0, /device:TPU:0, one launch (start us, length us, event | category | flops | bytes accessed | tf_op | source)
XLA Modules:
  0.0 579.3 jit_solution(17118914123731465109)
XLA Ops:
  6.6 1.3 reshape.133
  9.5 1.4 fusion.11
  11.8 1.5 fusion.37
  13.7 10.7 %select_reduce_fusion = (bf16[192,1920]{1,0:T(8,128)(2,1)}, bf16[192,1920]{1,0:T(8,128)(2,1)S(1)}) fusion(f32[192,8]{1,0:T(8,128)S(1)} %copy.59, f32[192,8]{1,0:T(8,128)S(1)} %copy.58), kind=kLoop, calls=%fused_computation.2 | loop fusion | flops 14008320 | bytes 1486848 | tf_op jit(solution)/shard_map/reduce_sum | solution.py:121
  24.3 6.5 %convolution_convert_fusion = bf16[1920,2048]{1,0:T(8,128)(2,1)} fusion(bf16[192,1920]{1,0:T(8,128)(2,1)S(1)} %get-tuple-element.6, bf16[192,2048]{1,0:T(8,128)(2,1)} %param.14, f32[2048]{0:T(1024)S(1)} %copy-done.9, f32[192]{0:T(256)S(1)} %add_rsqrt_fusion.2), kind=kOutput, calls=%fused_computation.6 | convolution fusion | flops 1515454464 | bytes 9396992 | tf_op jit(solution)/shard_map/dot_general | solution.py:122
  30.9 7.4 %all-to-all-start = ((bf16[16,120,2048]{2,1,0:T(8,128)(2,1)}), bf16[16,120,2048]{2,1,0:T(8,128)(2,1)}, u32[]{:S(2)}, u32[]{:S(2)}) async-start(bf16[16,120,2048]{2,1,0:T(8,128)(2,1)} %bitcast.60), calls=%async_computation | async-start | bytes 15728640 | tf_op jit(solution)/shard_map/all_to_all | solution.py:126
  39.0 197.1 %all-to-all-done = bf16[16,120,2048]{2,1,0:T(8,128)(2,1)} async-done(((bf16[16,120,2048]{2,1,0:T(8,128)(2,1)}), bf16[16,120,2048]{2,1,0:T(8,128)(2,1)}, u32[]{:S(2)}, u32[]{:S(2)}) %all-to-all-start) | async-done | bytes 7864352 | tf_op jit(solution)/shard_map/all_to_all | solution.py:126
  236.1 18.3 %fusion.1 = f32[16,120,1536]{2,1,0:T(8,128)} fusion(bf16[16,120,2048]{2,1,0:T(8,128)(2,1)} %all-to-all-done, bf16[1,2048,1536]{2,1,0:T(8,128)(2,1)} %param.24), kind=kOutput, calls=%fused_computation.7 | convolution fusion | flops 12079595520 | bytes 25952256 | tf_op jit(solution)/shard_map/ack,kf->acf/dot_general | solution.py:127
  254.4 9.3 %fusion.4 = f32[16,120,2048]{2,1,0:T(8,128)S(1)} fusion(bf16[1,768,2048]{2,1,0:T(8,128)(2,1)S(1)} %copy-done, f32[16,120,1536]{2,1,0:T(8,128)} %fusion.1), kind=kOutput, calls=%fused_computation.11 | convolution fusion | flops 6048645120 | bytes 30670848 | tf_op jit(solution)/shard_map/acf,fk->ack/dot_general | solution.py:131
  263.8 5.5 copy-done.2
  269.3 2.5 dynamic-slice_convert_fusion
  271.8 1.5 collective-permute-start
  273.3 86.2 %collective-permute-done = bf16[16,120,1024]{2,1,0:T(8,128)(2,1)} collective-permute-done((bf16[16,120,1024]{2,1,0:T(8,128)(2,1)}, bf16[16,120,1024]{2,1,0:T(8,128)(2,1)}, u32[]{:S(2)}, u32[]{:S(2)}) %collective-permute-start) | collective-permute-done | bytes 3932192 | tf_op jit(solution)/shard_map/ppermute | solution.py:19
  359.4 7.9 %add_convert_fusion = bf16[16,120,1024]{2,1,0:T(8,128)(2,1)} fusion(bf16[16,120,1024]{2,1,0:T(8,128)(2,1)} %collective-permute-done, f32[16,120,2048]{2,1,0:T(8,128)} %copy-done.2, s32[]{:T(128)S(6)} %select_n.53), kind=kLoop, calls=%fused_computation.4 | loop fusion | flops 5898240 | bytes 15728644 | tf_op jit(solution)/shard_map/convert_element_type | solution.py:137
  367.3 51.8 %all-to-all-start.1 = ((bf16[16,120,1024]{2,1,0:T(8,128)(2,1)}), bf16[16,120,1024]{2,1,0:T(8,128)(2,1)}, u32[]{:S(2)}, u32[]{:S(2)}) async-start(bf16[16,120,1024]{2,1,0:T(8,128)(2,1)} %add_convert_fusion), calls=%async_computation.1 | async-start | bytes 7864320 | tf_op jit(solution)/shard_map/all_to_all | solution.py:138
  420.7 2.2 fusion.34
  425.0 5.2 convolution_bitcast_fusion
  433.5 1.0 fusion.52
  435.4 1.4 copy.57
  436.8 55.4 %all-to-all-done.1 = bf16[16,120,1024]{2,1,0:T(8,128)(2,1)} async-done(((bf16[16,120,1024]{2,1,0:T(8,128)(2,1)}), bf16[16,120,1024]{2,1,0:T(8,128)(2,1)}, u32[]{:S(2)}, u32[]{:S(2)}) %all-to-all-start.1) | async-done | bytes 3932192 | tf_op jit(solution)/shard_map/all_to_all | solution.py:138
  492.2 4.0 fusion.53
  496.2 8.2 %fusion.9 = f32[192,2048]{1,0:T(8,128)} fusion(bf16[2048,2048]{1,0:T(8,128)(2,1)} %all-gather.8.cloned.1.call-done, f32[192,1024]{1,0:T(8,128)} %fusion.53, bf16[24,8,16,128]{3,2,1,0:T(8,128)(2,1)} %bitcast.64, pred[]{:T(512)S(6)} %eq.40), kind=kOutput, calls=%fused_computation.19 | convolution fusion | flops 1612185600 | bytes 11534337 | tf_op jit(solution)/shard_map/dot_general | solution.py:65
  504.4 65.7 %all-reduce.4.cloned.1.call-done = f32[192,2048]{1,0:T(8,128)} async-done(((f32[192,2048]{1,0:T(8,128)}), f32[192,2048]{1,0:T(8,128)}) %all-reduce.4.cloned.1.call-update) | async-done | bytes 1572880 | tf_op jit(solution)/shard_map/psum | solution.py:162
  570.1 2.7 fusion.17
  (69 shorter events, 11.2 us)
Async XLA Ops:
  6.5 247.9 %copy-start = (bf16[1,768,2048]{2,1,0:T(8,128)(2,1)S(1)}, bf16[1,768,2048]{2,1,0:T(8,128)(2,1)}, u32[]{:S(2)}) copy-start(bf16[1,768,2048]{2,1,0:T(8,128)(2,1)} %param.25) | copy-start | bytes 9437188
  6.5 6.8 %copy-start.7 = (s32[192,8]{0,1:T(8,128)S(1)}, s32[192,8]{0,1:T(8,128)}, u32[]{:S(2)}) copy-start(s32[192,8]{0,1:T(8,128)} %param.23) | copy-start | bytes 18436
  6.5 17.8 %copy-start.9 = (f32[2048]{0:T(1024)S(1)}, f32[2048]{0:T(1024)}, u32[]{:S(2)}) copy-start(f32[2048]{0:T(1024)} %param.16) | copy-start | bytes 24580
  6.5 414.1 %all-gather.4.cloned.1.call-start = ((), (), s32[]{:S(2)}) async-start(), calls=%async_computation.2 | async-start | bytes 2228224 | tf_op jit(solution)/shard_map/all_gather | solution.py:153
  8.7 416.3 %all-gather.6.cloned.1.call-start = ((), (), s32[]{:S(2)}) async-start(), calls=%async_computation.3 | async-start | bytes 8912896 | tf_op jit(solution)/shard_map/all_gather | solution.py:152
  30.9 205.3 %all-to-all-start = ((bf16[16,120,2048]{2,1,0:T(8,128)(2,1)}), bf16[16,120,2048]{2,1,0:T(8,128)(2,1)}, u32[]{:S(2)}, u32[]{:S(2)}) async-start(bf16[16,120,2048]{2,1,0:T(8,128)(2,1)} %bitcast.60), calls=%async_computation | async-start | bytes 15728640 | tf_op jit(solution)/shard_map/all_to_all | solution.py:126
  38.3 457.9 %all-gather.8.cloned.1.call-start = ((), (), s32[]{:S(2)}) async-start(), calls=%async_computation.4 | async-start | bytes 8912896 | tf_op jit(solution)/shard_map/all_gather | solution.py:154
  263.8 5.5 copy-start.2
  271.8 87.6 %collective-permute-start = (bf16[16,120,1024]{2,1,0:T(8,128)(2,1)}, bf16[16,120,1024]{2,1,0:T(8,128)(2,1)}, u32[]{:S(2)}, u32[]{:S(2)}) collective-permute-start(bf16[16,120,1024]{2,1,0:T(8,128)(2,1)} %dynamic-slice_convert_fusion), channel_id=1, source_target_pairs={{0,1},{1,0},{2,3},{3,2},{4,5},{5,4},{6,7},{7,6},{8,9},{9,8},{10,11... | collective-permute-start | bytes 11796488 | tf_op jit(solution)/shard_map/ppermute | solution.py:19
  367.3 52.8 %copy-start.3 = (bf16[192,2048]{1,0:T(8,128)(2,1)S(1)}, bf16[192,2048]{1,0:T(8,128)(2,1)}, u32[]{:S(2)}) copy-start(bf16[192,2048]{1,0:T(8,128)(2,1)} %param.13) | copy-start | bytes 2359300
  367.3 53.4 %copy-start.12 = (f32[2048]{0:T(1024)S(1)}, f32[2048]{0:T(1024)}, u32[]{:S(2)}) copy-start(f32[2048]{0:T(1024)} %param.15) | copy-start | bytes 24580
  367.3 124.9 %all-to-all-start.1 = ((bf16[16,120,1024]{2,1,0:T(8,128)(2,1)}), bf16[16,120,1024]{2,1,0:T(8,128)(2,1)}, u32[]{:S(2)}, u32[]{:S(2)}) async-start(bf16[16,120,1024]{2,1,0:T(8,128)(2,1)} %add_convert_fusion), calls=%async_computation.1 | async-start | bytes 7864320 | tf_op jit(solution)/shard_map/all_to_all | solution.py:138
  419.1 151.0 %all-reduce.4.cloned.1.call-start = ((), (), s32[]{:S(2)}) async-start(), calls=%async_computation.5 | async-start | bytes 3145728 | tf_op jit(solution)/shard_map/psum | solution.py:162
  420.0 4.1 copy-start.10
  430.3 1.0 copy-start.11
  431.7 1.1 copy-start.5
  432.6 0.9 copy-start.8
  433.5 1.0 copy-start.6
  434.6 57.7 %copy-start.4 = (bf16[192,1920]{1,0:T(8,128)(2,1)S(1)}, bf16[192,1920]{1,0:T(8,128)(2,1)}, u32[]{:S(2)}) copy-start(bf16[192,1920]{1,0:T(8,128)(2,1)} %get-tuple-element.5) | copy-start | bytes 2211844
  496.2 76.5 %copy-start.1 = (bf16[1,768,2048]{2,1,0:T(8,128)(2,1)S(1)}, bf16[1,768,2048]{2,1,0:T(8,128)(2,1)}, u32[]{:S(2)}) copy-start(bf16[1,768,2048]{2,1,0:T(8,128)(2,1)} %param.25) | copy-start | bytes 9437188
Sparse Core Ops, SparseCore 0:
  9.5 86.2 all-gather.3
  98.0 136.9 all-gather.5
  237.1 91.5 all-gather.7
  504.5 65.4 all-reduce.3
where the time goes:
time: 580 us; the launch traced here: 579 us
  waiting for transfers between devices  406 us (70%)
  starting transfers between devices  61.2 us (11%)
  matrix products  57 us (10%)
  other arithmetic  28.3 us (5%)
  local copies, waits for them, and re-layouts  13.7 us (2%)
  between operations  13.5 us (2%)
    all_to_all x1, waiting for transfers between devices, local(): lax.all_to_all(outgoing, 'ep', split_axis=0, concat_axis=0, tiled=True)  197 us
    ppermute x1, waiting for transfers between devices, from_partner(): return lax.ppermute(value, axis, pairs)  86.2 us
    psum x1, waiting for transfers between devices, local(): summed = lax.psum(total, 'tp')  65.7 us
    all_to_all x1, waiting for transfers between devices, local(): lax.all_to_all(expert_out, 'ep', split_axis=0, concat_axis=0, tiled=True)  55.4 us
    all_to_all x1, starting transfers between devices, local(): lax.all_to_all(expert_out, 'ep', split_axis=0, concat_axis=0, tiled=True)  51.8 us
    dot_general x1, matrix products, local(): jnp.einsum('ack,kf->acf', arrived, gate_up_weight[0], preferred_element_t...  18.3 us
  transfers between devices with their start and end apart: 7, of which 4 were waited for; matrix products, arithmetic and copies ran while one was open for 14% of the time, Pallas kernels for 0%

commit v1 on v0

--- a/solution.py
+++ b/solution.py
@@ -1,5 +1,7 @@
 import jax
 import jax.numpy as jnp
+from jax.experimental import pallas as pl
+from jax.experimental.pallas import tpu as pltpu
 from jax import lax
 from jax.sharding import PartitionSpec as P
 
@@ -67,7 +69,7 @@
     )
 
 
-def local(
+def weights_first(
     residual_in,
     shortcut,
     attn_gain,
@@ -163,7 +165,156 @@
     return (residual_in.astype(jnp.float32) + summed).astype(jnp.bfloat16)
 
 
+def rotary_tables(length, width):
+    half = width // 2
+    position = jnp.arange(length, dtype=jnp.float32)
+    freq = ROPE_BASE ** (-jnp.arange(half, dtype=jnp.float32) * 2.0 / width)
+    angle = position[:, None] * freq[None, :]
+    cosine, sine = jnp.cos(angle), jnp.sin(angle)
+    return jnp.concatenate([cosine, cosine], 1), jnp.concatenate([-sine, sine], 1)
+
+
+def spread_gates(moe_rows, router_weight, expert_ids):
+    experts = router_weight.shape[0]
+    logits = lax.dot_general(
+        moe_rows, router_weight, (((1,), (1,)), ((), ())), preferred_element_type=jnp.float32
+    )
+    hits = jnp.any(
+        expert_ids[:, :, None] == jnp.arange(experts, dtype=jnp.int32)[None, None, :], 1
+    )
+    scores = jnp.where(hits, jax.nn.sigmoid(logits), 0.0)
+    return scores / jnp.sum(scores, 1, keepdims=True)
+
+
+def rotated_norm(values, gain, cosine, sine):
+    wide = values * lax.rsqrt(jnp.mean(values * values, -1, keepdims=True) + EPS) * gain
+    return (wide * cosine + pltpu.roll(wide, HD // 2, 1) * sine).astype(jnp.bfloat16)
+
+
+def attend_head(qkv, query_gain, key_gain, cosine, sine):
+    seq = qkv.shape[0]
+    query = rotated_norm(qkv[:, :HD], query_gain, cosine, sine)
+    keys = rotated_norm(qkv[:, HD : 2 * HD], key_gain, cosine, sine)
+    values = qkv[:, 2 * HD :].astype(jnp.bfloat16)
+    logits = lax.dot_general(
+        query, keys, (((1,), (1,)), ((), ())), preferred_element_type=jnp.float32
+    ) * HD ** (-0.5)
+    below = lax.broadcasted_iota(jnp.int32, (seq, seq), 0) >= lax.broadcasted_iota(
+        jnp.int32, (seq, seq), 1
+    )
+    logits = jnp.where(below, logits, -1e30)
+    expo = jnp.exp(logits - jnp.max(logits, -1, keepdims=True))
+    probs = (expo / jnp.sum(expo, -1, keepdims=True)).astype(jnp.bfloat16)
+    return jnp.dot(probs, values, preferred_element_type=jnp.float32).astype(jnp.bfloat16)
+
+
+def heads_and_expert(
+    seq, attn_ref, moe_ref, qkv_ref, out_w_ref, up_ref, down_ref, qg_ref, kg_ref, cos_ref, sin_ref,
+    out_ref,
+):
+    d_model = attn_ref.shape[1]
+    ff_dev = down_ref.shape[0]
+    expert = lax.axis_index("ep")
+    qkv = jnp.dot(attn_ref[...], qkv_ref[...], preferred_element_type=jnp.float32)
+    parts = [
+        attend_head(qkv[at : at + seq], qg_ref[...], kg_ref[...], cos_ref[...], sin_ref[...])
+        for at in range(0, qkv.shape[0], seq)
+    ]
+    attended = jnp.concatenate(parts, 0)
+    gates = moe_ref[:, d_model:].astype(jnp.float32)
+    lane = lax.broadcasted_iota(jnp.int32, gates.shape, 1)
+    gate = jnp.sum(jnp.where(lane == expert, gates, 0.0), 1, keepdims=True)
+    paired = jnp.dot(moe_ref[:, :d_model], up_ref[...], preferred_element_type=jnp.float32)
+    front, back = paired[:, :ff_dev], paired[:, ff_dev:]
+    hidden = (front / (1.0 + jnp.exp(-front)) * back * gate).astype(jnp.bfloat16)
+    total = jnp.dot(hidden, down_ref[...], preferred_element_type=jnp.float32)
+    total += jnp.dot(attended, out_w_ref[...], preferred_element_type=jnp.float32)
+    out_ref[...] = total.astype(out_ref.dtype)
+
+
+def rows_first(
+    residual_in,
+    shortcut,
+    attn_gain,
+    moe_gain,
+    query_weight,
+    key_value,
+    output_weight,
+    query_gain,
+    key_gain,
+    router_weight,
+    expert_ids,
+    gate_up_weight,
+    down_weight,
+):
+    n_ep = lax.axis_size("ep")
+    n_tp = lax.axis_size("tp")
+    me, rank = lax.axis_index("ep"), lax.axis_index("tp")
+    rows, d_model = residual_in.shape
+    share = rows // n_tp
+    depth = key_value.shape[0]
+    residual = lax.dynamic_slice_in_dim(residual_in, rank * share, share, 0)
+    attn_rows = norm_rows(residual, attn_gain).astype(jnp.bfloat16)
+    moe_rows = norm_rows(
+        lax.dynamic_slice_in_dim(shortcut, rank * share, share, 0), moe_gain
+    ).astype(jnp.bfloat16)
+    ids = lax.dynamic_slice_in_dim(expert_ids, rank * share, share, 0)
+    gates = spread_gates(moe_rows, router_weight, ids).astype(jnp.bfloat16)
+    gates = jnp.pad(gates, ((0, 0), (0, HD - gates.shape[1])))
+    moe_rows = jnp.concatenate([moe_rows, gates], 1)
+    all_attn = lax.all_gather(attn_rows, ("ep", "tp"), axis=0, tiled=True)
+    all_moe = lax.all_gather(moe_rows, ("ep", "tp"), axis=0, tiled=True)
+
+    kv_count = KVH // n_tp
+    kv = lax.dynamic_slice_in_dim(
+        key_value.reshape(depth, 2, KVH, HD), rank * kv_count, kv_count, 2
+    )
+    kv = jnp.repeat(kv, n_ep // kv_count, 2).transpose(0, 2, 1, 3).reshape(depth, n_ep, 2 * HD)
+    sent = jnp.concatenate(
+        [query_weight.reshape(depth, n_ep, HD), kv, output_weight.reshape(depth, n_ep, HD)], 2
+    )
+    mine = lax.all_to_all(sent, "ep", split_axis=1, concat_axis=0, tiled=True)
+    mine = mine.reshape(d_model, 4 * HD)
+    cosine, sine = rotary_tables(rows, HD)
+    block = 2 * rows
+    whole = lambda *shape: pl.BlockSpec(shape, lambda i: (0,) * len(shape))
+    ff_dev = down_weight.shape[1]
+    total = n_ep * rows
+    partial_sum = pl.pallas_call(
+        lambda *refs: heads_and_expert(rows, *refs),
+        grid=(total // block,),
+        in_specs=[
+            pl.BlockSpec((block, d_model), lambda i: (i, 0)),
+            pl.BlockSpec((block, d_model + HD), lambda i: (i, 0)),
+            whole(d_model, 3 * HD),
+            whole(HD, d_model),
+            whole(d_model, 2 * ff_dev),
+            whole(ff_dev, d_model),
+            whole(1, HD),
+            whole(1, HD),
+            whole(rows, HD),
+            whole(rows, HD),
+        ],
+        out_specs=pl.BlockSpec((block, d_model), lambda i: (i, 0)),
+        out_shape=jax.ShapeDtypeStruct((total, d_model), jnp.bfloat16),
+        compiler_params=pltpu.CompilerParams(vmem_limit_bytes=56 * 2**20),
+        cost_estimate=pl.CostEstimate(
+            flops=2 * total * d_model * (3 * ff_dev + 4 * HD),
+            bytes_accessed=total * d_model * 6 + 3 * ff_dev * d_model * 2,
+            transcendentals=total * ff_dev,
+        ),
+    )(
+        all_attn, all_moe, mine[:, : 3 * HD], mine[:, 3 * HD :].T, gate_up_weight[0],
+        down_weight[0], query_gain[None], key_gain[None], cosine, sine,
+    )
+    summed = lax.psum_scatter(partial_sum, ("ep", "tp"), scatter_dimension=0, tiled=True)
+    out = (residual.astype(jnp.float32) + summed.astype(jnp.float32)).astype(jnp.bfloat16)
+    return lax.all_gather(out, "tp", axis=0, tiled=True)
+
+
 def solution(mesh):
+    n_ep, n_tp = mesh.shape["ep"], mesh.shape["tp"]
+    local = rows_first if n_ep * n_tp == QH and n_tp == 2 else weights_first
     return jax.shard_map(
         local,
         mesh=mesh,

time: 580 us -> 466 us (0.80)
  matrix products: 57 us -> 0.34 us
  starting transfers between devices: 61.2 us -> 7.45 us
  Pallas kernels: 0 us -> 53.3 us
  waiting for transfers between devices: 406 us -> 361 us
  other arithmetic: 28.3 us -> 10 us
  blocking collectives: 0 us -> 10.1 us
    all_to_all x2 -> x1, waiting for transfers between devices: 253 us -> 61.2 us  [rows_first(): mine = lax.all_to_all(sent, 'ep', split_axis=1, concat_axis=0, tiled=True)]
    reduce_scatter x0 -> x1, waiting for transfers between devices: none -> 154 us  [rows_first(): lax.psum_scatter(partial_sum, ('ep', 'tp'), scatter_dimension=0, tiled=True)]
    all_gather x3 -> x2, waiting for transfers between devices: 0.02 us -> 146 us  [the longest x1 101 us: rows_first(): all_moe = lax.all_gather(moe_rows, ('ep', 'tp'), axis=0, tiled=True)]
    ppermute x1 -> x0, waiting for transfers between devices: 86.2 us -> none  [from_partner(): return lax.ppermute(value, axis, pairs)]
    psum x1 -> x0, waiting for transfers between devices: 65.7 us -> none  [local(): summed = lax.psum(total, 'tp')]
    dot_general x11 -> x1, matrix products: 57 us -> 0.34 us  [spread_gates(): lax.dot_general(moe_rows, router_weight, (((1,), (1,)), ((), ())), prefer...]
    pallas_call x0 -> x1, Pallas kernels: none -> 53.3 us  [rows_first(): pl.pallas_call(lambda *refs: heads_and_expert(rows, *refs), grid=(total /...]
    all_to_all x2 -> x1, starting transfers between devices: 59.2 us -> 7.36 us  [rows_first(): mine = lax.all_to_all(sent, 'ep', split_axis=1, concat_axis=0, tiled=True)]
  transfers between devices with their start and end apart: 7 -> 4, of which waited for: 4 -> 4; matrix products, arithmetic and copies ran while one was open for 14% -> 3% of each run, Pallas kernels for 0% -> 0%
where the time goes in v1:
time: 466 us; the launch traced here: 465 us
  waiting for transfers between devices  361 us (77%)
  Pallas kernels  53.3 us (11%)
  between operations  13.3 us (3%)
  blocking collectives  10.1 us (2%)
  other arithmetic  10 us (2%)
  local copies, waits for them, and re-layouts  9.57 us (2%)
  starting transfers between devices  7.45 us (2%)
    reduce_scatter x1, waiting for transfers between devices, rows_first(): lax.psum_scatter(partial_sum, ('ep', 'tp'), scatter_dimension=0, tiled=True)  154 us
    all_gather x1, waiting for transfers between devices, rows_first(): all_moe = lax.all_gather(moe_rows, ('ep', 'tp'), axis=0, tiled=True)  101 us
    all_to_all x1, waiting for transfers between devices, rows_first(): mine = lax.all_to_all(sent, 'ep', split_axis=1, concat_axis=0, tiled=True)  61.2 us
    pallas_call x1, Pallas kernels, rows_first(): pl.pallas_call(lambda *refs: heads_and_expert(rows, *refs), grid=(total /...  53.3 us
    all_gather x1, waiting for transfers between devices, rows_first(): all_attn = lax.all_gather(attn_rows, ('ep', 'tp'), axis=0, tiled=True)  45.5 us
    all_gather x1, blocking collectives, rows_first(): return lax.all_gather(out, 'tp', axis=0, tiled=True)  10.1 us
  transfers between devices with their start and end apart: 4, of which 4 were waited for; matrix products, arithmetic and copies ran while one was open for 3% of the time, Pallas kernels for 0%

profile of v1, /device:TPU:0, one launch (start us, length us, event | category | flops | bytes accessed | tf_op | source)
XLA Modules:
  0.0 465.5 jit_solution(6979597489233442707)
XLA Ops:
  6.5 1.2 fusion.8
  7.8 2.0 fusion.10
  9.9 0.8 constant_dynamic-slice_fusion.1
  10.8 1.2 fusion.5
  12.0 0.9 fusion.7
  12.9 0.3 fusion.17
  13.4 0.8 fusion.12
  15.5 1.5 pad_maximum_fusion
  17.0 7.4 %all-to-all-start = ((bf16[128,16,512]{0,2,1:T(8,128)(2,1)}), bf16[128,16,512]{0,2,1:T(8,128)(2,1)S(1)}, u32[]{:S(2)}, u32[]{:S(2)}) async-start(bf16[128,16,512]{0,2,1:T(8,128)(2,1)} %pad_maximum_fusion), calls=%async_computation | async-start | bytes 4194304 | tf_op jit(solution)/shard_map/all_to_all | solution.py:276
  24.4 0.4 fusion.16
  24.8 0.8 pad_maximum_fusion.1
  25.6 61.2 %all-to-all-done = bf16[128,16,512]{0,2,1:T(8,128)(2,1)S(1)} async-done(((bf16[128,16,512]{0,2,1:T(8,128)(2,1)}), bf16[128,16,512]{0,2,1:T(8,128)(2,1)S(1)}, u32[]{:S(2)}, u32[]{:S(2)}) %all-to-all-start) | async-done | bytes 2097184 | tf_op jit(solution)/shard_map/all_to_all | solution.py:276
  86.8 1.4 copy.32
  88.2 0.5 copy.37
  88.8 1.2 slice.8
  90.0 2.6 copy.33.refs_2_
  92.6 0.8 slice_bitcast_fusion.refs_3_
  93.4 45.5 %all-gather.3.cloned.1.call-done.refs_0_ = bf16[3072,2048]{1,0:T(8,128)(2,1)} async-done(((bf16[96,2048]{1,0:T(8,128)(2,1)}), bf16[3072,2048]{1,0:T(8,128)(2,1)}) %all-gather.3.cloned.1.call-update) | async-done | bytes 12582928 | tf_op jit(solution)/shard_map/all_gather | solution.py:265
  138.9 100.9 %all-gather.5.cloned.1.call-done.refs_1_ = bf16[3072,2176]{1,0:T(8,128)(2,1)} async-done(((bf16[96,2176]{1,0:T(8,128)(2,1)}), bf16[3072,2176]{1,0:T(8,128)(2,1)}) %all-gather.5.cloned.1.call-update) | async-done | bytes 13369360 | tf_op jit(solution)/shard_map/all_gather | solution.py:266
  239.8 53.3 %shard_map.127 = bf16[3072,2048]{1,0:T(8,128)(2,1)} custom-call(bf16[3072,2048]{1,0:T(8,128)(2,1)} %all-gather.3.cloned.1.call-done.refs_0_, bf16[3072,2176]{1,0:T(8,128)(2,1)} %all-gather.5.cloned.1.call-done.refs_1_, bf16[2048,384]{1,0:T(8,128)(2,1)} %copy.33.refs_2_, bf16[128,2048]{1,0:T(8,128)(2,1)} %slice_bitcast_fusion.refs_3_, ...), custom_call_target="tpu_custom_call" | custom-call | flops 35433480192 | bytes 47185920 | tf_op jit(solution)/shard_map/pallas_call | solution.py:283
  293.1 153.7 %reduce-scatter.2.cloned.1.call-done = bf16[96,2048]{1,0:T(8,128)(2,1)} async-done(((bf16[3072,2048]{1,0:T(8,128)(2,1)}), bf16[96,2048]{1,0:T(8,128)(2,1)}) %reduce-scatter.2.cloned.1.call-update) | async-done | bytes 393232 | tf_op jit(solution)/shard_map/reduce_scatter | solution.py:310
  446.9 1.1 fusion.11
  448.0 10.1 %all_gather.11 = bf16[192,2048]{1,0:T(8,128)(2,1)S(1)} all-gather(bf16[96,2048]{1,0:T(8,128)(2,1)S(1)} %fusion.11), channel_id=1, replica_groups=mesh['ep'=16,'tp'=2] {'tp'}, dimensions={0}, use_global_device_ids=true | all-gather | bytes 1179648 | tf_op jit(solution)/shard_map/all_gather | solution.py:312
  458.1 0.9 copy.40
  (32 shorter events, 1.6 us)
Async XLA Ops:
  6.5 6.4 %copy-start = (bf16[16,2048]{1,0:T(8,128)(2,1)S(1)}, bf16[16,2048]{1,0:T(8,128)(2,1)}, u32[]{:S(2)}) copy-start(bf16[16,2048]{1,0:T(8,128)(2,1)} %param.22) | copy-start | bytes 196612
  6.5 5.5 %copy-start.3 = (bf16[192,2048]{1,0:T(8,128)(2,1)S(1)}, bf16[192,2048]{1,0:T(8,128)(2,1)}, u32[]{:S(2)}) copy-start(bf16[192,2048]{1,0:T(8,128)(2,1)} %param.14) | copy-start | bytes 2359300
  6.5 132.3 %all-gather.3.cloned.1.call-start = ((), (), s32[]{:S(2)}) async-start(), calls=%async_computation.2 | async-start | bytes 12976128 | tf_op jit(solution)/shard_map/all_gather | solution.py:265
  7.8 6.4 %copy-start.6 = (bf16[128,1024]{1,0:T(8,128)(2,1)S(1)}, bf16[128,1024]{1,0:T(8,128)(2,1)}, u32[]{:S(2)}) copy-start(bf16[128,1024]{1,0:T(8,128)(2,1)} %param.18) | copy-start | bytes 786436
  9.8 230.0 %all-gather.5.cloned.1.call-start = ((), (), s32[]{:S(2)}) async-start(), calls=%async_computation.3 | async-start | bytes 13787136 | tf_op jit(solution)/shard_map/all_gather | solution.py:266
  10.8 3.9 copy-start.4
  12.9 2.0 copy-start.5
  17.0 69.9 %all-to-all-start = ((bf16[128,16,512]{0,2,1:T(8,128)(2,1)}), bf16[128,16,512]{0,2,1:T(8,128)(2,1)S(1)}, u32[]{:S(2)}, u32[]{:S(2)}) async-start(bf16[128,16,512]{0,2,1:T(8,128)(2,1)} %pad_maximum_fusion), calls=%async_computation | async-start | bytes 4194304 | tf_op jit(solution)/shard_map/all_to_all | solution.py:276
  24.3 422.5 %reduce-scatter.2.cloned.1.call-start = ((), (), s32[]{:S(2)}) async-start(), calls=%async_computation.4 | async-start | bytes 12976128 | tf_op jit(solution)/shard_map/reduce_scatter | solution.py:310
  293.1 153.7 %copy-start.2 = (bf16[192,2048]{1,0:T(8,128)(2,1)S(1)}, bf16[192,2048]{1,0:T(8,128)(2,1)}, u32[]{:S(2)}) copy-start(bf16[192,2048]{1,0:T(8,128)(2,1)} %param.13) | copy-start | bytes 2359300
  293.1 165.8 %copy-start.1 = (bf16[16,2048]{1,0:T(8,128)(2,1)S(1)}, bf16[16,2048]{1,0:T(8,128)(2,1)}, u32[]{:S(2)}) copy-start(bf16[16,2048]{1,0:T(8,128)(2,1)} %param.22) | copy-start | bytes 196612
Sparse Core Ops, SparseCore 0:
  10.3 128.5 all-gather.2
  141.8 97.9 all-gather.4
  293.3 153.5 reduce-scatter.1

commit v2 on v1

--- a/solution.py
+++ b/solution.py
@@ -208,26 +208,42 @@
     return jnp.dot(probs, values, preferred_element_type=jnp.float32).astype(jnp.bfloat16)
 
 
-def heads_and_expert(
-    seq, attn_ref, moe_ref, qkv_ref, out_w_ref, up_ref, down_ref, qg_ref, kg_ref, cos_ref, sin_ref,
-    out_ref,
+def half_expert(moe_ref, up_ref, down_ref):
+    d_model = up_ref.shape[0]
+    ff_dev = down_ref.shape[0]
+    gates = moe_ref[:, d_model:].astype(jnp.float32)
+    lane = lax.broadcasted_iota(jnp.int32, gates.shape, 1)
+    gate = jnp.sum(jnp.where(lane == lax.axis_index("ep"), gates, 0.0), 1, keepdims=True)
+    paired = jnp.dot(moe_ref[:, :d_model], up_ref[...], preferred_element_type=jnp.float32)
+    front, back = paired[:, :ff_dev], paired[:, ff_dev:]
+    hidden = (front / (1.0 + jnp.exp(-front)) * back * gate).astype(jnp.bfloat16)
+    return jnp.dot(hidden, down_ref[...], preferred_element_type=jnp.float32)
+
+
+def own_half(moe_ref, up_ref, down_ref, out_ref):
+    out_ref[...] = half_expert(moe_ref, up_ref, down_ref)
+
+
+def heads_and_half(
+    seq, attn_ref, moe_ref, before_ref, qkv_ref, out_w_ref, up_ref, down_ref, qg_ref, kg_ref,
+    cos_ref, sin_ref, out_ref,
 ):
-    d_model = attn_ref.shape[1]
-    ff_dev = down_ref.shape[0]
-    expert = lax.axis_index("ep")
     qkv = jnp.dot(attn_ref[...], qkv_ref[...], preferred_element_type=jnp.float32)
     parts = [
-        attend_head(qkv[at : at + seq], qg_ref[...], kg_ref[...], cos_ref[...], sin_ref[...])
+        jnp.concatenate(
+            [
+                attend_head(
+                    qkv[at : at + seq, head : head + 3 * HD],
+                    qg_ref[...], kg_ref[...], cos_ref[...], sin_ref[...],
+                )
+                for head in range(0, qkv.shape[1], 3 * HD)
+            ],
+            1,
+        )
         for at in range(0, qkv.shape[0], seq)
     ]
     attended = jnp.concatenate(parts, 0)
-    gates = moe_ref[:, d_model:].astype(jnp.float32)
-    lane = lax.broadcasted_iota(jnp.int32, gates.shape, 1)
-    gate = jnp.sum(jnp.where(lane == expert, gates, 0.0), 1, keepdims=True)
-    paired = jnp.dot(moe_ref[:, :d_model], up_ref[...], preferred_element_type=jnp.float32)
-    front, back = paired[:, :ff_dev], paired[:, ff_dev:]
-    hidden = (front / (1.0 + jnp.exp(-front)) * back * gate).astype(jnp.bfloat16)
-    total = jnp.dot(hidden, down_ref[...], preferred_element_type=jnp.float32)
+    total = before_ref[...] + half_expert(moe_ref, up_ref, down_ref)
     total += jnp.dot(attended, out_w_ref[...], preferred_element_type=jnp.float32)
     out_ref[...] = total.astype(out_ref.dtype)
 
@@ -250,20 +266,25 @@
     n_ep = lax.axis_size("ep")
     n_tp = lax.axis_size("tp")
     me, rank = lax.axis_index("ep"), lax.axis_index("tp")
+    side = me % 2
     rows, d_model = residual_in.shape
-    share = rows // n_tp
+    share = rows // 2
     depth = key_value.shape[0]
-    residual = lax.dynamic_slice_in_dim(residual_in, rank * share, share, 0)
-    attn_rows = norm_rows(residual, attn_gain).astype(jnp.bfloat16)
-    moe_rows = norm_rows(
-        lax.dynamic_slice_in_dim(shortcut, rank * share, share, 0), moe_gain
-    ).astype(jnp.bfloat16)
-    ids = lax.dynamic_slice_in_dim(expert_ids, rank * share, share, 0)
-    gates = spread_gates(moe_rows, router_weight, ids).astype(jnp.bfloat16)
+    their_up = from_partner(gate_up_weight, "tp", 0)
+    their_down = from_partner(down_weight, "tp", 0)
+
+    attn_rows = norm_rows(residual_in, attn_gain).astype(jnp.bfloat16)
+    moe_rows = norm_rows(shortcut, moe_gain).astype(jnp.bfloat16)
+    gates = spread_gates(moe_rows, router_weight, expert_ids).astype(jnp.bfloat16)
     gates = jnp.pad(gates, ((0, 0), (0, HD - gates.shape[1])))
-    moe_rows = jnp.concatenate([moe_rows, gates], 1)
-    all_attn = lax.all_gather(attn_rows, ("ep", "tp"), axis=0, tiled=True)
-    all_moe = lax.all_gather(moe_rows, ("ep", "tp"), axis=0, tiled=True)
+    joined = jnp.concatenate([moe_rows, gates, attn_rows], 1)
+    away = lax.dynamic_slice_in_dim(joined, (1 - side) * share, share, 0)
+    kept = lax.dynamic_slice_in_dim(joined, side * share, share, 0)
+    givers = [(at * n_tp + at % 2, (at ^ 1) * n_tp + at % 2) for at in range(n_ep)]
+    given = lax.ppermute(away, ("ep", "tp"), givers)
+    piece = jnp.where(side == rank, kept, given)
+    all_moe = lax.all_gather(piece[:, : d_model + HD], "ep", axis=0, tiled=True)
+    all_attn = lax.all_gather(piece[:, d_model + HD :], "ep", axis=0, tiled=True)
 
     kv_count = KVH // n_tp
     kv = lax.dynamic_slice_in_dim(
@@ -275,19 +296,40 @@
     )
     mine = lax.all_to_all(sent, "ep", split_axis=1, concat_axis=0, tiled=True)
     mine = mine.reshape(d_model, 4 * HD)
+    theirs = from_partner(mine, "tp", 0)
+    qkv = jnp.concatenate([mine[:, : 3 * HD], theirs[:, : 3 * HD]], 1)
+    out_w = jnp.concatenate([mine[:, 3 * HD :], theirs[:, 3 * HD :]], 1).T
+
     cosine, sine = rotary_tables(rows, HD)
     block = 2 * rows
     whole = lambda *shape: pl.BlockSpec(shape, lambda i: (0,) * len(shape))
+    tiles = lambda width: pl.BlockSpec((block, width), lambda i: (i, 0))
     ff_dev = down_weight.shape[1]
-    total = n_ep * rows
+    total = n_ep * share
+    expert_flops = 6 * total * d_model * ff_dev
+    params = pltpu.CompilerParams(vmem_limit_bytes=56 * 2**20)
+    before = pl.pallas_call(
+        own_half,
+        grid=(total // block,),
+        in_specs=[tiles(d_model + HD), whole(d_model, 2 * ff_dev), whole(ff_dev, d_model)],
+        out_specs=tiles(d_model),
+        out_shape=jax.ShapeDtypeStruct((total, d_model), jnp.float32),
+        compiler_params=params,
+        cost_estimate=pl.CostEstimate(
+            flops=expert_flops,
+            bytes_accessed=total * d_model * 6 + 3 * ff_dev * d_model * 2,
+            transcendentals=total * ff_dev,
+        ),
+    )(all_moe, gate_up_weight[0], down_weight[0])
     partial_sum = pl.pallas_call(
-        lambda *refs: heads_and_expert(rows, *refs),
+        lambda *refs: heads_and_half(rows, *refs),
         grid=(total // block,),
         in_specs=[
-            pl.BlockSpec((block, d_model), lambda i: (i, 0)),
-            pl.BlockSpec((block, d_model + HD), lambda i: (i, 0)),
-            whole(d_model, 3 * HD),
-            whole(HD, d_model),
+            tiles(d_model),
+            tiles(d_model + HD),
+            tiles(d_model),
+            whole(d_model, 6 * HD),
+            whole(2 * HD, d_model),
             whole(d_model, 2 * ff_dev),
             whole(ff_dev, d_model),
             whole(1, HD),
@@ -295,21 +337,27 @@
             whole(rows, HD),
             whole(rows, HD),
         ],
-        out_specs=pl.BlockSpec((block, d_model), lambda i: (i, 0)),
+        out_specs=tiles(d_model),
         out_shape=jax.ShapeDtypeStruct((total, d_model), jnp.bfloat16),
-        compiler_params=pltpu.CompilerParams(vmem_limit_bytes=56 * 2**20),
+        compiler_params=params,
         cost_estimate=pl.CostEstimate(
-            flops=2 * total * d_model * (3 * ff_dev + 4 * HD),
-            bytes_accessed=total * d_model * 6 + 3 * ff_dev * d_model * 2,
+            flops=expert_flops + 16 * total * d_model * HD,
+            bytes_accessed=total * d_model * 10 + 3 * ff_dev * d_model * 2,
             transcendentals=total * ff_dev,
         ),
     )(
-        all_attn, all_moe, mine[:, : 3 * HD], mine[:, 3 * HD :].T, gate_up_weight[0],
-        down_weight[0], query_gain[None], key_gain[None], cosine, sine,
-    )
-    summed = lax.psum_scatter(partial_sum, ("ep", "tp"), scatter_dimension=0, tiled=True)
-    out = (residual.astype(jnp.float32) + summed.astype(jnp.float32)).astype(jnp.bfloat16)
-    return lax.all_gather(out, "tp", axis=0, tiled=True)
+        all_attn, all_moe, before, qkv, out_w, their_up[0], their_down[0],
+        query_gain[None], key_gain[None], cosine, sine,
+    )
+    summed = lax.psum_scatter(partial_sum, "ep", scatter_dimension=0, tiled=True)
+    across = lax.ppermute(summed, "ep", [(at, at ^ 1) for at in range(n_ep)])
+    low = jnp.where(side == 0, summed, across)
+    high = jnp.where(side == 0, across, summed)
+    sequence = jnp.concatenate([low, high], 0)
+    owners = [(at * n_tp + at % 2, at * n_tp + 1 - at % 2) for at in range(n_ep)]
+    handed = lax.ppermute(sequence, ("ep", "tp"), owners)
+    summed = jnp.where(side == rank, sequence, handed)
+    return (residual_in.astype(jnp.float32) + summed.astype(jnp.float32)).astype(jnp.bfloat16)
 
 
 def solution(mesh):

time: 466 us -> 431 us (0.925)
  waiting for transfers between devices: 361 us -> 313 us
  blocking collectives: 10.1 us -> 0 us
  starting transfers between devices: 7.45 us -> 16.9 us
  Pallas kernels: 53.3 us -> 61.6 us
    ppermute x0 -> x6, waiting for transfers between devices: none -> 168 us  [the longest x3 155 us: from_partner(): return lax.ppermute(value, axis, pairs)]
    all_gather x2, waiting for transfers between devices: 146 us -> 0.01 us  [the longest x1 0.01 us: rows_first(): all_moe = lax.all_gather(piece[:, :d_model + HD], 'ep', axis=0, tiled=True)]
    reduce_scatter x1, waiting for transfers between devices: 154 us -> 86.7 us  [rows_first(): lax.psum_scatter(partial_sum, 'ep', scatter_dimension=0, tiled=True)]
    all_gather x1 -> x0, blocking collectives: 10.1 us -> none  [rows_first(): return lax.all_gather(out, 'tp', axis=0, tiled=True)]
    ppermute x0 -> x6, starting transfers between devices: none -> 10 us  [the longest x3 4.2 us: from_partner(): return lax.ppermute(value, axis, pairs)]
    pallas_call x1 -> x2, Pallas kernels: 53.3 us -> 61.6 us  [the longest x1 40.4 us: rows_first(): pl.pallas_call(lambda *refs: heads_and_half(rows, *refs), grid=(total //...]
  transfers between devices with their start and end apart: 4 -> 10, of which waited for: 4 -> 7; matrix products, arithmetic and copies ran while one was open for 3% -> 3% of each run, Pallas kernels for 0% -> 5%
where the time goes in v2:
time: 431 us
  waiting for transfers between devices  313 us (73%)
  Pallas kernels  61.6 us (14%)
  starting transfers between devices  16.9 us (4%)
  between operations  13.4 us (3%)
  other arithmetic  12.6 us (3%)
  local copies, waits for them, and re-layouts  12.4 us (3%)
    ppermute x3, waiting for transfers between devices, from_partner(): return lax.ppermute(value, axis, pairs)  155 us
    reduce_scatter x1, waiting for transfers between devices, rows_first(): lax.psum_scatter(partial_sum, 'ep', scatter_dimension=0, tiled=True)  86.7 us
    all_to_all x1, waiting for transfers between devices, rows_first(): mine = lax.all_to_all(sent, 'ep', split_axis=1, concat_axis=0, tiled=True)  58.5 us
    pallas_call x1, Pallas kernels, rows_first(): pl.pallas_call(lambda *refs: heads_and_half(rows, *refs), grid=(total //...  40.4 us
    pallas_call x1, Pallas kernels, rows_first(): pl.pallas_call(own_half, grid=(total // block,), in_specs=[tiles(d_model...  21.3 us
    ppermute x1, waiting for transfers between devices, rows_first(): handed = lax.ppermute(sequence, ('ep', 'tp'), owners)  9.44 us
  transfers between devices with their start and end apart: 10, of which 7 were waited for; matrix products, arithmetic and copies ran while one was open for 3% of the time, Pallas kernels for 5%

profile of v2, /device:TPU:0, one launch (start us, length us, event | category | flops | bytes accessed | tf_op | source)
XLA Modules:
  0.0 430.7 jit_solution(618095793145975626)
XLA Ops:
  6.6 1.5 fusion.4
  8.1 1.4 fusion.7
  10.3 1.1 fusion.6
  12.3 2.4 collective-permute-start
  14.7 1.9 collective-permute-done
  18.5 1.1 reshape.46
  20.7 1.5 pad_maximum_fusion.1
  22.2 6.8 %all-to-all-start = ((bf16[128,16,512]{0,2,1:T(8,128)(2,1)}), bf16[128,16,512]{0,2,1:T(8,128)(2,1)S(1)}, u32[]{:S(2)}, u32[]{:S(2)}) async-start(bf16[128,16,512]{0,2,1:T(8,128)(2,1)} %pad_maximum_fusion.1), calls=%async_computation | async-start | bytes 4194304 | tf_op jit(solution)/shard_map/all_to_all | solution.py:297
  29.0 2.1 collective-permute-start.2
  31.1 58.5 %all-to-all-done = bf16[128,16,512]{0,2,1:T(8,128)(2,1)S(1)} async-done(((bf16[128,16,512]{0,2,1:T(8,128)(2,1)}), bf16[128,16,512]{0,2,1:T(8,128)(2,1)S(1)}, u32[]{:S(2)}, u32[]{:S(2)}) %all-to-all-start) | async-done | bytes 2097184 | tf_op jit(solution)/shard_map/all_to_all | solution.py:297
  89.6 1.4 copy.32
  91.5 1.5 collective-permute-start.1
  95.7 116.9 %collective-permute-done.1 = bf16[2048,512]{0,1:T(8,128)(2,1)S(1)} collective-permute-done((bf16[2048,512]{0,1:T(8,128)(2,1)S(1)}, bf16[2048,512]{0,1:T(8,128)(2,1)S(1)}, u32[]{:S(2)}, u32[]{:S(2)}) %collective-permute-start.1) | collective-permute-done | bytes 2097184 | tf_op jit(solution)/shard_map/ppermute | solution.py:21
  212.6 1.3 copy-done.5
  214.3 3.1 copy.33.refs_3_
  218.5 2.1 maximum_bitcast_fusion.refs_4_
  220.6 21.3 %shard_map.127.refs_2_ = f32[1536,2048]{1,0:T(8,128)} custom-call(bf16[1536,2176]{1,0:T(8,128)(2,1)} %all-gather.5.cloned.1.call-done.moe_ref.refs_1_, bf16[2048,1536]{1,0:T(8,128)(2,1)} %bitcast.35, bf16[768,2048]{1,0:T(8,128)(2,1)} %bitcast.1.down_ref), custom_call_target="tpu_custom_call" | custom-call | flops 14495514624 | bytes 28311552 | tf_op jit(solution)/shard_map/pallas_call | solution.py:311
  241.8 38.0 %collective-permute-done.3 = bf16[1,768,2048]{2,1,0:T(8,128)(2,1)} collective-permute-done((bf16[1,768,2048]{2,1,0:T(8,128)(2,1)}, bf16[1,768,2048]{2,1,0:T(8,128)(2,1)}, u32[]{:S(2)}, u32[]{:S(2)}) %collective-permute-start.3) | collective-permute-done | bytes 3145760 | tf_op jit(solution)/shard_map/ppermute | solution.py:21
  279.9 40.4 %shard_map.128 = bf16[1536,2048]{1,0:T(8,128)(2,1)} custom-call(bf16[1536,2048]{1,0:T(8,128)(2,1)} %all-gather.3.cloned.1.call-done.refs_0_, bf16[1536,2176]{1,0:T(8,128)(2,1)} %all-gather.5.cloned.1.call-done.moe_ref.refs_1_, f32[1536,2048]{1,0:T(8,128)} %shard_map.127.refs_2_, bf16[2048,768]{1,0:T(8,128)(2,1)} %copy.33.refs_3_, ...), custom_call_target="tpu_custom_call" | custom-call | flops 20937965568 | bytes 40894464 | tf_op jit(solution)/shard_map/pallas_call | solution.py:324
  320.3 86.7 %reduce-scatter.2.cloned.1.call-done = bf16[96,2048]{1,0:T(8,128)(2,1)} async-done(((bf16[1536,2048]{1,0:T(8,128)(2,1)}), bf16[96,2048]{1,0:T(8,128)(2,1)}) %reduce-scatter.2.cloned.1.call-update) | async-done | bytes 393232 | tf_op jit(solution)/shard_map/reduce_scatter | solution.py:352
  407.0 1.9 collective-permute-done.4
  410.0 3.4 collective-permute-start.5
  413.5 9.4 %collective-permute-done.5 = bf16[192,2048]{1,0:T(8,128)(2,1)S(1)} collective-permute-done((bf16[192,2048]{1,0:T(8,128)(2,1)S(1)}, bf16[192,2048]{1,0:T(8,128)(2,1)S(1)}, u32[]{:S(2)}, u32[]{:S(2)}) %collective-permute-start.5) | collective-permute-done | bytes 786464 | tf_op jit(solution)/shard_map/ppermute | solution.py:358
  422.9 1.3 fusion.10
  (53 shorter events, 10.5 us)
Async XLA Ops:
  6.5 4.9 %copy-start = (bf16[16,2048]{1,0:T(8,128)(2,1)S(1)}, bf16[16,2048]{1,0:T(8,128)(2,1)}, u32[]{:S(2)}) copy-start(bf16[16,2048]{1,0:T(8,128)(2,1)} %param.22) | copy-start | bytes 196612
  6.5 3.8 copy-start.4
  6.5 3.8 copy-start.2
  6.5 214.0 %all-gather.5.cloned.1.call-start = ((), (), s32[]{:S(2)}) async-start(), calls=%async_computation.3 | async-start | bytes 7102464 | tf_op jit(solution)/shard_map/all_gather | solution.py:286
  12.3 4.3 collective-permute-start
  16.8 3.1 copy-start.6
  16.8 3.4 copy-start.7
  17.6 262.3 %all-gather.3.cloned.1.call-start = ((), (), s32[]{:S(2)}) async-start(), calls=%async_computation.2 | async-start | bytes 6684672 | tf_op jit(solution)/shard_map/all_gather | solution.py:287
  22.2 67.4 %all-to-all-start = ((bf16[128,16,512]{0,2,1:T(8,128)(2,1)}), bf16[128,16,512]{0,2,1:T(8,128)(2,1)S(1)}, u32[]{:S(2)}, u32[]{:S(2)}) async-start(bf16[128,16,512]{0,2,1:T(8,128)(2,1)} %pad_maximum_fusion.1), calls=%async_computation | async-start | bytes 4194304 | tf_op jit(solution)/shard_map/all_to_all | solution.py:297
  29.0 378.0 %reduce-scatter.2.cloned.1.call-start = ((), (), s32[]{:S(2)}) async-start(), calls=%async_computation.4 | async-start | bytes 6684672 | tf_op jit(solution)/shard_map/reduce_scatter | solution.py:352
  29.0 250.9 %collective-permute-start.2 = (bf16[1,2048,1536]{2,1,0:T(8,128)(2,1)}, bf16[1,2048,1536]{2,1,0:T(8,128)(2,1)}, u32[]{:S(2)}, u32[]{:S(2)}) collective-permute-start(bf16[1,2048,1536]{2,1,0:T(8,128)(2,1)} %param.24), channel_id=1, source_target_pairs={{0,1},{1,0},{2,3},{3,2},{4,5},{5,4},{6,7},{7,6},{8,9},{9,8},{10,11... | collective-permute-start | bytes 18874376 | tf_op jit(solution)/shard_map/ppermute | solution.py:21
  91.5 121.1 %collective-permute-start.1 = (bf16[2048,512]{0,1:T(8,128)(2,1)S(1)}, bf16[2048,512]{0,1:T(8,128)(2,1)S(1)}, u32[]{:S(2)}, u32[]{:S(2)}) collective-permute-start(bf16[2048,512]{0,1:T(8,128)(2,1)S(1)} %bitcast.27), channel_id=1, source_target_pairs={{0,1},{1,0},{2,3},{3,2},{4,5},{5,4},{6,7},{7,6},{8,9},{9,8},{10,11... | collective-permute-start | bytes 6291464 | tf_op jit(solution)/shard_map/ppermute | solution.py:21
  93.0 186.9 %collective-permute-start.3 = (bf16[1,768,2048]{2,1,0:T(8,128)(2,1)}, bf16[1,768,2048]{2,1,0:T(8,128)(2,1)}, u32[]{:S(2)}, u32[]{:S(2)}) collective-permute-start(bf16[1,768,2048]{2,1,0:T(8,128)(2,1)} %param.25), channel_id=1, source_target_pairs={{0,1},{1,0},{2,3},{3,2},{4,5},{5,4},{6,7},{7,6},{8,9},{9,8},{10,11... | collective-permute-start | bytes 9437192 | tf_op jit(solution)/shard_map/ppermute | solution.py:21
  212.6 1.3 copy-start.5
  320.3 102.6 %copy-start.3 = (bf16[192,2048]{1,0:T(8,128)(2,1)S(1)}, bf16[192,2048]{1,0:T(8,128)(2,1)}, u32[]{:S(2)}) copy-start(bf16[192,2048]{1,0:T(8,128)(2,1)} %param.13) | copy-start | bytes 2359300
  407.0 1.9 collective-permute-start.4
  410.0 14.2 %copy-start.1 = (bf16[16,2048]{1,0:T(8,128)(2,1)S(1)}, bf16[16,2048]{1,0:T(8,128)(2,1)}, u32[]{:S(2)}) copy-start(bf16[16,2048]{1,0:T(8,128)(2,1)} %param.22) | copy-start | bytes 196612
  410.0 12.9 %collective-permute-start.5 = (bf16[192,2048]{1,0:T(8,128)(2,1)S(1)}, bf16[192,2048]{1,0:T(8,128)(2,1)S(1)}, u32[]{:S(2)}, u32[]{:S(2)}) collective-permute-start(bf16[192,2048]{1,0:T(8,128)(2,1)S(1)} %pad_maximum_fusion.2), channel_id=1, source_target_pairs={{0,1},{3,2},{4,5},{7,6},{8,9},{11,10},{12,13},{15,14},{16,17},{19,... | collective-permute-start | bytes 2359304 | tf_op jit(solution)/shard_map/ppermute | solution.py:358
Sparse Core Ops, SparseCore 0:
  17.7 101.7 all-gather.4
  121.8 60.7 all-gather.2
  320.4 86.5 reduce-scatter.1

commit v3 on v2

--- a/solution.py
+++ b/solution.py
@@ -224,9 +224,13 @@
     out_ref[...] = half_expert(moe_ref, up_ref, down_ref)
 
 
-def heads_and_half(
-    seq, attn_ref, moe_ref, before_ref, qkv_ref, out_w_ref, up_ref, down_ref, qg_ref, kg_ref,
-    cos_ref, sin_ref, out_ref,
+def other_half(moe_ref, before_ref, up_ref, down_ref, out_ref):
+    total = before_ref[...] + half_expert(moe_ref, up_ref, down_ref)
+    out_ref[...] = total.astype(out_ref.dtype)
+
+
+def two_heads(
+    seq, attn_ref, before_ref, qkv_ref, out_w_ref, qg_ref, kg_ref, cos_ref, sin_ref, out_ref
 ):
     qkv = jnp.dot(attn_ref[...], qkv_ref[...], preferred_element_type=jnp.float32)
     parts = [
@@ -243,9 +247,9 @@
         for at in range(0, qkv.shape[0], seq)
     ]
     attended = jnp.concatenate(parts, 0)
-    total = before_ref[...] + half_expert(moe_ref, up_ref, down_ref)
-    total += jnp.dot(attended, out_w_ref[...], preferred_element_type=jnp.float32)
-    out_ref[...] = total.astype(out_ref.dtype)
+    out_ref[...] = before_ref[...] + jnp.dot(
+        attended, out_w_ref[...], preferred_element_type=jnp.float32
+    )
 
 
 def rows_first(
@@ -287,18 +291,15 @@
     all_attn = lax.all_gather(piece[:, d_model + HD :], "ep", axis=0, tiled=True)
 
     kv_count = KVH // n_tp
-    kv = lax.dynamic_slice_in_dim(
-        key_value.reshape(depth, 2, KVH, HD), rank * kv_count, kv_count, 2
-    )
-    kv = jnp.repeat(kv, n_ep // kv_count, 2).transpose(0, 2, 1, 3).reshape(depth, n_ep, 2 * HD)
+    pairs = key_value.reshape(depth, 2, n_tp, kv_count, HD)
+    kv = jnp.where(rank == 0, pairs, pairs[:, :, ::-1]).transpose(0, 3, 2, 1, 4)
+    kv = jnp.repeat(kv.reshape(depth, kv_count, 4 * HD), n_ep // kv_count, 1)
     sent = jnp.concatenate(
-        [query_weight.reshape(depth, n_ep, HD), kv, output_weight.reshape(depth, n_ep, HD)], 2
+        [query_weight.reshape(depth, n_ep, HD), output_weight.reshape(depth, n_ep, HD), kv], 2
     )
     mine = lax.all_to_all(sent, "ep", split_axis=1, concat_axis=0, tiled=True)
-    mine = mine.reshape(d_model, 4 * HD)
-    theirs = from_partner(mine, "tp", 0)
-    qkv = jnp.concatenate([mine[:, : 3 * HD], theirs[:, : 3 * HD]], 1)
-    out_w = jnp.concatenate([mine[:, 3 * HD :], theirs[:, 3 * HD :]], 1).T
+    mine = mine.reshape(d_model, 6 * HD)
+    theirs = from_partner(mine[:, : 2 * HD], "tp", 0)
 
     cosine, sine = rotary_tables(rows, HD)
     block = 2 * rows
@@ -321,34 +322,54 @@
             transcendentals=total * ff_dev,
         ),
     )(all_moe, gate_up_weight[0], down_weight[0])
-    partial_sum = pl.pallas_call(
-        lambda *refs: heads_and_half(rows, *refs),
+    theirs, before = lax.optimization_barrier((theirs, before))
+    qkv = jnp.concatenate(
+        [mine[:, :HD], mine[:, 2 * HD : 4 * HD], theirs[:, :HD], mine[:, 4 * HD :]], 1
+    )
+    out_w = jnp.concatenate([mine[:, HD : 2 * HD], theirs[:, HD:]], 1).T
+    before = pl.pallas_call(
+        lambda *refs: two_heads(rows, *refs),
         grid=(total // block,),
         in_specs=[
             tiles(d_model),
-            tiles(d_model + HD),
             tiles(d_model),
             whole(d_model, 6 * HD),
             whole(2 * HD, d_model),
-            whole(d_model, 2 * ff_dev),
-            whole(ff_dev, d_model),
             whole(1, HD),
             whole(1, HD),
             whole(rows, HD),
             whole(rows, HD),
         ],
         out_specs=tiles(d_model),
+        out_shape=jax.ShapeDtypeStruct((total, d_model), jnp.float32),
+        compiler_params=params,
+        cost_estimate=pl.CostEstimate(
+            flops=16 * total * d_model * HD,
+            bytes_accessed=total * d_model * 10 + 8 * HD * d_model * 2,
+            transcendentals=total * rows * 2,
+        ),
+    )(
+        all_attn, before, qkv, out_w, query_gain[None], key_gain[None], cosine, sine,
+    )
+    their_up, their_down, before = lax.optimization_barrier((their_up, their_down, before))
+    partial_sum = pl.pallas_call(
+        other_half,
+        grid=(total // block,),
+        in_specs=[
+            tiles(d_model + HD),
+            tiles(d_model),
+            whole(d_model, 2 * ff_dev),
+            whole(ff_dev, d_model),
+        ],
+        out_specs=tiles(d_model),
         out_shape=jax.ShapeDtypeStruct((total, d_model), jnp.bfloat16),
         compiler_params=params,
         cost_estimate=pl.CostEstimate(
-            flops=expert_flops + 16 * total * d_model * HD,
-            bytes_accessed=total * d_model * 10 + 3 * ff_dev * d_model * 2,
+            flops=expert_flops,
+            bytes_accessed=total * d_model * 8 + 3 * ff_dev * d_model * 2,
             transcendentals=total * ff_dev,
         ),
-    )(
-        all_attn, all_moe, before, qkv, out_w, their_up[0], their_down[0],
-        query_gain[None], key_gain[None], cosine, sine,
-    )
+    )(all_moe, before, their_up[0], their_down[0])
     summed = lax.psum_scatter(partial_sum, "ep", scatter_dimension=0, tiled=True)
     across = lax.ppermute(summed, "ep", [(at, at ^ 1) for at in range(n_ep)])
     low = jnp.where(side == 0, summed, across)

time: 431 us -> 418 us (0.970)
  waiting for transfers between devices: 313 us -> 296 us
    ppermute x3, waiting for transfers between devices: 155 us -> 103 us  [from_partner(): return lax.ppermute(value, axis, pairs)]
    all_to_all x1, waiting for transfers between devices: 58.5 us -> 92.5 us  [rows_first(): mine = lax.all_to_all(sent, 'ep', split_axis=1, concat_axis=0, tiled=True)]
    pallas_call x1 -> x2, Pallas kernels: 40.4 us -> 42.9 us  [the longest x1 21.8 us: rows_first(): pl.pallas_call(other_half, grid=(total // block,), in_specs=[tiles(d_mode...]
  transfers between devices with their start and end apart: 10 -> 10, of which waited for: 7 -> 6; matrix products, arithmetic and copies ran while one was open for 3% -> 4% of each run, Pallas kernels for 5% -> 10%
where the time goes in v3:
time: 418 us
  waiting for transfers between devices  296 us (71%)
  Pallas kernels  64.5 us (15%)
  starting transfers between devices  16.3 us (4%)
  other arithmetic  13.9 us (3%)
  local copies, waits for them, and re-layouts  13.7 us (3%)
  between operations  13.3 us (3%)
    ppermute x3, waiting for transfers between devices, from_partner(): return lax.ppermute(value, axis, pairs)  103 us
    all_to_all x1, waiting for transfers between devices, rows_first(): mine = lax.all_to_all(sent, 'ep', split_axis=1, concat_axis=0, tiled=True)  92.5 us
    reduce_scatter x1, waiting for transfers between devices, rows_first(): lax.psum_scatter(partial_sum, 'ep', scatter_dimension=0, tiled=True)  86.7 us
    pallas_call x1, Pallas kernels, rows_first(): pl.pallas_call(other_half, grid=(total // block,), in_specs=[tiles(d_mode...  21.8 us
    pallas_call x1, Pallas kernels, rows_first(): pl.pallas_call(own_half, grid=(total // block,), in_specs=[tiles(d_model...  21.6 us
    pallas_call x1, Pallas kernels, rows_first(): pl.pallas_call(lambda *refs: two_heads(rows, *refs), grid=(total // block...  21.1 us
    ppermute x1, waiting for transfers between devices, rows_first(): handed = lax.ppermute(sequence, ('ep', 'tp'), owners)  9.44 us
  transfers between devices with their start and end apart: 10, of which 6 were waited for; matrix products, arithmetic and copies ran while one was open for 4% of the time, Pallas kernels for 10%

profile of v3, /device:TPU:0, one launch (start us, length us, event | category | flops | bytes accessed | tf_op | source)
XLA Modules:
  0.0 417.9 jit_solution(10368631011131109149)
XLA Ops:
  6.5 1.4 fusion.7
  8.0 1.4 fusion.4
  10.2 1.8 fusion.6
  12.8 2.4 collective-permute-start
  15.2 1.9 collective-permute-done
  21.2 1.9 pad_maximum_fusion
  23.1 6.8 %all-to-all-start = ((bf16[128,16,768]{0,2,1:T(8,128)(2,1)}), bf16[128,16,768]{0,2,1:T(8,128)(2,1)S(1)}, u32[]{:S(2)}, u32[]{:S(2)}) async-start(bf16[128,16,768]{0,2,1:T(8,128)(2,1)} %pad_maximum_fusion), calls=%async_computation | async-start | bytes 6291456 | tf_op jit(solution)/shard_map/all_to_all | solution.py:300
  30.0 2.1 collective-permute-start.1
  33.4 92.5 %all-to-all-done = bf16[128,16,768]{0,2,1:T(8,128)(2,1)S(1)} async-done(((bf16[128,16,768]{0,2,1:T(8,128)(2,1)}), bf16[128,16,768]{0,2,1:T(8,128)(2,1)S(1)}, u32[]{:S(2)}, u32[]{:S(2)}) %all-to-all-start) | async-done | bytes 3145760 | tf_op jit(solution)/shard_map/all_to_all | solution.py:300
  125.8 2.0 copy.47
  127.9 1.3 copy.52
  129.2 1.7 fusion.21
  132.0 1.4 collective-permute-start.3
  133.4 21.6 %shard_map.127.refs_1_ = f32[1536,2048]{1,0:T(8,128)} custom-call(bf16[1536,2176]{1,0:T(8,128)(2,1)} %all-gather.3.cloned.1.call-done.moe_ref, bf16[2048,1536]{1,0:T(8,128)(2,1)} %bitcast.38, bf16[768,2048]{1,0:T(8,128)(2,1)} %bitcast.39), custom_call_target="tpu_custom_call" | custom-call | flops 14495514624 | bytes 28311552 | tf_op jit(solution)/shard_map/pallas_call | solution.py:312
  155.0 103.3 %collective-permute-done.3 = bf16[2048,256]{0,1:T(8,128)(2,1)S(1)} collective-permute-done((bf16[2048,256]{0,1:T(8,128)(2,1)S(1)}, bf16[2048,256]{0,1:T(8,128)(2,1)S(1)}, u32[]{:S(2)}, u32[]{:S(2)}) %collective-permute-start.3) | collective-permute-done | bytes 1048608 | tf_op jit(solution)/shard_map/ppermute | solution.py:21
  259.4 2.8 copy.48.refs_2_
  262.3 2.3 maximum_bitcast_fusion.refs_3_
  264.6 21.1 %shard_map.128.before_ref = f32[1536,2048]{1,0:T(8,128)} custom-call(bf16[1536,2048]{1,0:T(8,128)(2,1)} %all-gather.5.cloned.1.call-done.refs_0_, f32[1536,2048]{1,0:T(8,128)} %shard_map.127.refs_1_, bf16[2048,768]{1,0:T(8,128)(2,1)} %copy.48.refs_2_, bf16[256,2048]{1,0:T(8,128)(2,1)} %maximum_bitcast_fusion.refs_3_, f32[1,128]{1,0:T(1,128)} %bitcast.36, ...), custom_call_target="tpu_custom_call" | custom-call | flops 6442450944 | bytes 35651584 | tf_op jit(solution)/shard_map/pallas_call | solution.py:330
  285.6 21.8 %shard_map.129 = bf16[1536,2048]{1,0:T(8,128)(2,1)} custom-call(bf16[1536,2176]{1,0:T(8,128)(2,1)} %all-gather.3.cloned.1.call-done.moe_ref, f32[1536,2048]{1,0:T(8,128)} %shard_map.128.before_ref, bf16[2048,1536]{1,0:T(8,128)(2,1)} %bitcast.13.up_ref, bf16[768,2048]{1,0:T(8,128)(2,1)} %bitcast.14.down_ref), custom_call_target="tpu_custom_call" | custom-call | flops 14495514624 | bytes 34603008 | tf_op jit(solution)/shard_map/pallas_call | solution.py:355
  307.5 86.7 %reduce-scatter.2.cloned.1.call-done = bf16[96,2048]{1,0:T(8,128)(2,1)} async-done(((bf16[1536,2048]{1,0:T(8,128)(2,1)}), bf16[96,2048]{1,0:T(8,128)(2,1)}) %reduce-scatter.2.cloned.1.call-update) | async-done | bytes 393232 | tf_op jit(solution)/shard_map/reduce_scatter | solution.py:373
  394.2 1.9 collective-permute-done.4
  397.2 3.4 collective-permute-start.5
  400.6 9.4 %collective-permute-done.5 = bf16[192,2048]{1,0:T(8,128)(2,1)S(1)} collective-permute-done((bf16[192,2048]{1,0:T(8,128)(2,1)S(1)}, bf16[192,2048]{1,0:T(8,128)(2,1)S(1)}, u32[]{:S(2)}, u32[]{:S(2)}) %collective-permute-start.5) | collective-permute-done | bytes 786464 | tf_op jit(solution)/shard_map/ppermute | solution.py:379
  410.1 1.3 fusion.10
  (53 shorter events, 10.4 us)
Async XLA Ops:
  6.5 5.5 %copy-start = (bf16[16,2048]{1,0:T(8,128)(2,1)S(1)}, bf16[16,2048]{1,0:T(8,128)(2,1)}, u32[]{:S(2)}) copy-start(bf16[16,2048]{1,0:T(8,128)(2,1)} %param.22) | copy-start | bytes 196612
  6.5 126.9 %all-gather.3.cloned.1.call-start = ((), (), s32[]{:S(2)}) async-start(), calls=%async_computation.2 | async-start | bytes 7102464 | tf_op jit(solution)/shard_map/all_gather | solution.py:290
  12.8 4.3 %collective-permute-start = (bf16[96,4224]{1,0:T(8,128)(2,1)S(1)}, bf16[96,4224]{1,0:T(8,128)(2,1)S(1)}, u32[]{:S(2)}, u32[]{:S(2)}) collective-permute-start(bf16[96,4224]{1,0:T(8,128)(2,1)S(1)} %constant_dynamic-slice_fusion), channel_id=1, source_target_pairs={{0,2},{3,1},{4,6},{7,5},{8,10},{11,9},{12,14},{15,13},{16,18},{19,... | collective-permute-start | bytes 2433032 | tf_op jit(solution)/shard_map/ppermute | solution.py:288
  17.3 2.9 copy-start.6
  17.3 3.2 copy-start.7
  18.1 246.4 %all-gather.5.cloned.1.call-start = ((), (), s32[]{:S(2)}) async-start(), calls=%async_computation.3 | async-start | bytes 6684672 | tf_op jit(solution)/shard_map/all_gather | solution.py:291
  23.1 102.7 %all-to-all-start = ((bf16[128,16,768]{0,2,1:T(8,128)(2,1)}), bf16[128,16,768]{0,2,1:T(8,128)(2,1)S(1)}, u32[]{:S(2)}, u32[]{:S(2)}) async-start(bf16[128,16,768]{0,2,1:T(8,128)(2,1)} %pad_maximum_fusion), calls=%async_computation | async-start | bytes 6291456 | tf_op jit(solution)/shard_map/all_to_all | solution.py:300
  29.9 364.2 %reduce-scatter.2.cloned.1.call-start = ((), (), s32[]{:S(2)}) async-start(), calls=%async_computation.4 | async-start | bytes 6684672 | tf_op jit(solution)/shard_map/reduce_scatter | solution.py:373
  30.0 255.7 %collective-permute-start.1 = (bf16[1,2048,1536]{2,1,0:T(8,128)(2,1)}, bf16[1,2048,1536]{2,1,0:T(8,128)(2,1)}, u32[]{:S(2)}, u32[]{:S(2)}) collective-permute-start(bf16[1,2048,1536]{2,1,0:T(8,128)(2,1)} %param.24), channel_id=1, source_target_pairs={{0,1},{1,0},{2,3},{3,2},{4,5},{5,4},{6,7},{7,6},{8,9},{9,8},{10,11... | collective-permute-start | bytes 18874376 | tf_op jit(solution)/shard_map/ppermute | solution.py:21
  32.1 253.5 %collective-permute-start.2 = (bf16[1,768,2048]{2,1,0:T(8,128)(2,1)}, bf16[1,768,2048]{2,1,0:T(8,128)(2,1)}, u32[]{:S(2)}, u32[]{:S(2)}) collective-permute-start(bf16[1,768,2048]{2,1,0:T(8,128)(2,1)} %param.25), channel_id=1, source_target_pairs={{0,1},{1,0},{2,3},{3,2},{4,5},{5,4},{6,7},{7,6},{8,9},{9,8},{10,11... | collective-permute-start | bytes 9437192 | tf_op jit(solution)/shard_map/ppermute | solution.py:21
  132.0 126.3 %collective-permute-start.3 = (bf16[2048,256]{0,1:T(8,128)(2,1)S(1)}, bf16[2048,256]{0,1:T(8,128)(2,1)S(1)}, u32[]{:S(2)}, u32[]{:S(2)}) collective-permute-start(bf16[2048,256]{0,1:T(8,128)(2,1)S(1)} %get-tuple-element.19), channel_id=1, source_target_pairs={{0,1},{1,0},{2,3},{3,2},{4,5},{5,4},{6,7},{7,6},{8,9},{9,8},{10,11... | collective-permute-start | bytes 3145736 | tf_op jit(solution)/shard_map/ppermute | solution.py:21
  133.4 125.7 %copy-start.3 = (bf16[2048,256]{0,1:T(8,128)(2,1)S(1)}, bf16[2048,256]{0,1:T(8,128)(2,1)}, u32[]{:S(2)}) copy-start(bf16[2048,256]{0,1:T(8,128)(2,1)} %get-tuple-element.17) | copy-start | bytes 3145732
  133.4 125.7 %copy-start.4 = (bf16[2048,256]{0,1:T(8,128)(2,1)S(1)}, bf16[2048,256]{0,1:T(8,128)(2,1)}, u32[]{:S(2)}) copy-start(bf16[2048,256]{0,1:T(8,128)(2,1)} %get-tuple-element.18) | copy-start | bytes 3145732
  133.4 125.7 %copy-start.5 = (bf16[2048,128]{0,1:T(8,128)(2,1)S(1)}, bf16[2048,128]{0,1:T(8,128)(2,1)}, u32[]{:S(2)}) copy-start(bf16[2048,128]{0,1:T(8,128)(2,1)} %get-tuple-element.16) | copy-start | bytes 1572868
  307.5 102.6 %copy-start.2 = (bf16[192,2048]{1,0:T(8,128)(2,1)S(1)}, bf16[192,2048]{1,0:T(8,128)(2,1)}, u32[]{:S(2)}) copy-start(bf16[192,2048]{1,0:T(8,128)(2,1)} %param.13) | copy-start | bytes 2359300
  394.2 1.9 collective-permute-start.4
  394.2 17.2 %copy-start.1 = (bf16[16,2048]{1,0:T(8,128)(2,1)S(1)}, bf16[16,2048]{1,0:T(8,128)(2,1)}, u32[]{:S(2)}) copy-start(bf16[16,2048]{1,0:T(8,128)(2,1)} %param.22) | copy-start | bytes 196612
  397.2 12.9 %collective-permute-start.5 = (bf16[192,2048]{1,0:T(8,128)(2,1)S(1)}, bf16[192,2048]{1,0:T(8,128)(2,1)S(1)}, u32[]{:S(2)}, u32[]{:S(2)}) collective-permute-start(bf16[192,2048]{1,0:T(8,128)(2,1)S(1)} %pad_maximum_fusion.2), channel_id=1, source_target_pairs={{0,1},{3,2},{4,5},{7,6},{8,9},{11,10},{12,13},{15,14},{16,17},{19,... | collective-permute-start | bytes 2359304 | tf_op jit(solution)/shard_map/ppermute | solution.py:379
Sparse Core Ops, SparseCore 0:
  18.3 113.7 all-gather.2
  134.3 64.5 all-gather.4
  307.6 86.5 reduce-scatter.1

commit v4 on v3

--- a/solution.py
+++ b/solution.py
@@ -237,10 +237,12 @@
         jnp.concatenate(
             [
                 attend_head(
-                    qkv[at : at + seq, head : head + 3 * HD],
+                    jnp.concatenate(
+                        [qkv[at : at + seq, head : head + HD], qkv[at : at + seq, 2 * HD :]], 1
+                    ),
                     qg_ref[...], kg_ref[...], cos_ref[...], sin_ref[...],
                 )
-                for head in range(0, qkv.shape[1], 3 * HD)
+                for head in (0, HD)
             ],
             1,
         )
@@ -274,6 +276,8 @@
     rows, d_model = residual_in.shape
     share = rows // 2
     depth = key_value.shape[0]
+    own_w = jnp.stack([query_weight, output_weight])
+    their_w = from_partner(own_w, "tp", 0)
     their_up = from_partner(gate_up_weight, "tp", 0)
     their_down = from_partner(down_weight, "tp", 0)
 
@@ -290,16 +294,14 @@
     all_moe = lax.all_gather(piece[:, : d_model + HD], "ep", axis=0, tiled=True)
     all_attn = lax.all_gather(piece[:, d_model + HD :], "ep", axis=0, tiled=True)
 
-    kv_count = KVH // n_tp
-    pairs = key_value.reshape(depth, 2, n_tp, kv_count, HD)
-    kv = jnp.where(rank == 0, pairs, pairs[:, :, ::-1]).transpose(0, 3, 2, 1, 4)
-    kv = jnp.repeat(kv.reshape(depth, kv_count, 4 * HD), n_ep // kv_count, 1)
-    sent = jnp.concatenate(
-        [query_weight.reshape(depth, n_ep, HD), output_weight.reshape(depth, n_ep, HD), kv], 2
-    )
+    kv = key_value.reshape(depth, 2, KVH, HD).transpose(0, 2, 1, 3)
+    kv = jnp.repeat(kv.reshape(depth, KVH, 2 * HD), n_ep // KVH, 1)
+    low = jnp.where(rank == 0, own_w, their_w)
+    high = jnp.where(rank == 0, their_w, own_w)
+    both = jnp.concatenate([low, high], 2).reshape(2, depth, n_ep, 2 * HD)
+    sent = jnp.concatenate([both[0], both[1], kv], 2)
     mine = lax.all_to_all(sent, "ep", split_axis=1, concat_axis=0, tiled=True)
     mine = mine.reshape(d_model, 6 * HD)
-    theirs = from_partner(mine[:, : 2 * HD], "tp", 0)
 
     cosine, sine = rotary_tables(rows, HD)
     block = 2 * rows
@@ -322,18 +324,15 @@
             transcendentals=total * ff_dev,
         ),
     )(all_moe, gate_up_weight[0], down_weight[0])
-    theirs, before = lax.optimization_barrier((theirs, before))
-    qkv = jnp.concatenate(
-        [mine[:, :HD], mine[:, 2 * HD : 4 * HD], theirs[:, :HD], mine[:, 4 * HD :]], 1
-    )
-    out_w = jnp.concatenate([mine[:, HD : 2 * HD], theirs[:, HD:]], 1).T
+    qkv = jnp.concatenate([mine[:, : 2 * HD], mine[:, 4 * HD :]], 1)
+    out_w = mine[:, 2 * HD : 4 * HD].T
     before = pl.pallas_call(
         lambda *refs: two_heads(rows, *refs),
         grid=(total // block,),
         in_specs=[
             tiles(d_model),
             tiles(d_model),
-            whole(d_model, 6 * HD),
+            whole(d_model, 4 * HD),
             whole(2 * HD, d_model),
             whole(1, HD),
             whole(1, HD),
@@ -344,7 +343,7 @@
         out_shape=jax.ShapeDtypeStruct((total, d_model), jnp.float32),
         compiler_params=params,
         cost_estimate=pl.CostEstimate(
-            flops=16 * total * d_model * HD,
+            flops=12 * total * d_model * HD,
             bytes_accessed=total * d_model * 10 + 8 * HD * d_model * 2,
             transcendentals=total * rows * 2,
         ),

time: 418 us -> 393 us (0.940)
  waiting for transfers between devices: 296 us -> 275 us
    ppermute x3, waiting for transfers between devices: 103 us -> 68.3 us  [from_partner(): return lax.ppermute(value, axis, pairs)]
    all_gather x1, waiting for transfers between devices: 0.01 us -> 30.2 us  [rows_first(): all_attn = lax.all_gather(piece[:, d_model + HD:], 'ep', axis=0, tiled=True)]
    all_to_all x1, waiting for transfers between devices: 92.5 us -> 78.1 us  [rows_first(): mine = lax.all_to_all(sent, 'ep', split_axis=1, concat_axis=0, tiled=True)]
  transfers between devices with their start and end apart: 10 -> 10, of which waited for: 6 -> 8; matrix products, arithmetic and copies ran while one was open for 4% -> 4% of each run, Pallas kernels for 10% -> 10%
where the time goes in v4:
time: 393 us
  waiting for transfers between devices  275 us (70%)
  Pallas kernels  60.6 us (15%)
  starting transfers between devices  19.7 us (5%)
  between operations  13.3 us (3%)
  local copies, waits for them, and re-layouts  12.6 us (3%)
  other arithmetic  11.1 us (3%)
    reduce_scatter x1, waiting for transfers between devices, rows_first(): lax.psum_scatter(partial_sum, 'ep', scatter_dimension=0, tiled=True)  85.6 us
    all_to_all x1, waiting for transfers between devices, rows_first(): mine = lax.all_to_all(sent, 'ep', split_axis=1, concat_axis=0, tiled=True)  78.1 us
    ppermute x3, waiting for transfers between devices, from_partner(): return lax.ppermute(value, axis, pairs)  68.3 us
    all_gather x1, waiting for transfers between devices, rows_first(): all_attn = lax.all_gather(piece[:, d_model + HD:], 'ep', axis=0, tiled=True)  30.2 us
    pallas_call x1, Pallas kernels, rows_first(): pl.pallas_call(other_half, grid=(total // block,), in_specs=[tiles(d_mode...  21.8 us
    pallas_call x1, Pallas kernels, rows_first(): pl.pallas_call(own_half, grid=(total // block,), in_specs=[tiles(d_model...  21.3 us
    pallas_call x1, Pallas kernels, rows_first(): pl.pallas_call(lambda *refs: two_heads(rows, *refs), grid=(total // block...  17.5 us
    ppermute x1, waiting for transfers between devices, rows_first(): handed = lax.ppermute(sequence, ('ep', 'tp'), owners)  9.44 us
  transfers between devices with their start and end apart: 10, of which 8 were waited for; matrix products, arithmetic and copies ran while one was open for 4% of the time, Pallas kernels for 10%

profile of v4, /device:TPU:0, one launch (start us, length us, event | category | flops | bytes accessed | tf_op | source)
XLA Modules:
  0.0 392.6 jit_solution(3518902354853327740)
XLA Ops:
  6.6 1.5 fusion.7
  8.1 1.4 fusion.4
  12.3 3.3 collective-permute-start
  15.5 1.2 collective-permute-done
  18.7 4.1 %collective-permute-start.3 = (bf16[2,128,2048]{2,1,0:T(8,128)(2,1)S(1)}, bf16[2,128,2048]{2,1,0:T(8,128)(2,1)S(1)}, u32[]{:S(2)}, u32[]{:S(2)}) collective-permute-start(bf16[2,128,2048]{2,1,0:T(8,128)(2,1)S(1)} %pad_maximum_fusion.3), channel_id=1, source_target_pairs={{0,1},{1,0},{2,3},{3,2},{4,5},{5,4},{6,7},{7,6},{8,9},{9,8},{10,11... | collective-permute-start | bytes 3145736 | tf_op jit(solution)/shard_map/ppermute | solution.py:21
  24.7 20.7 %collective-permute-done.3 = bf16[2,128,2048]{2,1,0:T(8,128)(2,1)S(1)} collective-permute-done((bf16[2,128,2048]{2,1,0:T(8,128)(2,1)S(1)}, bf16[2,128,2048]{2,1,0:T(8,128)(2,1)S(1)}, u32[]{:S(2)}, u32[]{:S(2)}) %collective-permute-start.3) | collective-permute-done | bytes 1048608 | tf_op jit(solution)/shard_map/ppermute | solution.py:21
  47.2 1.8 pad_maximum_fusion
  49.0 6.7 %all-to-all-start = ((bf16[128,16,768]{0,2,1:T(8,128)(2,1)}), bf16[128,16,768]{0,2,1:T(8,128)(2,1)S(1)}, u32[]{:S(2)}, u32[]{:S(2)}) async-start(bf16[128,16,768]{0,2,1:T(8,128)(2,1)} %pad_maximum_fusion), calls=%async_computation | async-start | bytes 6291456 | tf_op jit(solution)/shard_map/all_to_all | solution.py:303
  56.5 1.3 collective-permute-start.2
  59.1 78.1 %all-to-all-done = bf16[128,16,768]{0,2,1:T(8,128)(2,1)S(1)} async-done(((bf16[128,16,768]{0,2,1:T(8,128)(2,1)}), bf16[128,16,768]{0,2,1:T(8,128)(2,1)S(1)}, u32[]{:S(2)}, u32[]{:S(2)}) %all-to-all-start) | async-done | bytes 3145760 | tf_op jit(solution)/shard_map/all_to_all | solution.py:303
  137.2 2.0 copy.47
  139.2 1.3 copy.52
  140.5 1.4 slice_bitcast_fusion
  142.1 2.7 copy.48.refs_2_
  144.8 21.3 %shard_map.127.refs_1_ = f32[1536,2048]{1,0:T(8,128)} custom-call(bf16[1536,2176]{1,0:T(8,128)(2,1)} %all-gather.3.cloned.1.call-done.moe_ref, bf16[2048,1536]{1,0:T(8,128)(2,1)} %bitcast.43, bf16[768,2048]{1,0:T(8,128)(2,1)} %bitcast.44), custom_call_target="tpu_custom_call" | custom-call | flops 14495514624 | bytes 28311552 | tf_op jit(solution)/shard_map/pallas_call | solution.py:314
  166.1 30.2 %all-gather.5.cloned.1.call-done.refs_0_ = bf16[1536,2048]{1,0:T(8,128)(2,1)} async-done(((bf16[96,2048]{1,0:T(8,128)(2,1)}), bf16[1536,2048]{1,0:T(8,128)(2,1)}) %all-gather.5.cloned.1.call-update) | async-done | bytes 6291472 | tf_op jit(solution)/shard_map/all_gather | solution.py:295
  196.3 17.5 %shard_map.128.before_ref = f32[1536,2048]{1,0:T(8,128)} custom-call(bf16[1536,2048]{1,0:T(8,128)(2,1)} %all-gather.5.cloned.1.call-done.refs_0_, f32[1536,2048]{1,0:T(8,128)} %shard_map.127.refs_1_, bf16[2048,512]{1,0:T(8,128)(2,1)} %copy.48.refs_2_, bf16[256,2048]{1,0:T(8,128)(2,1)} %get-tuple-element.11.refs_3_, f32[1,128]{1,0:T(1,128)} %bitcast.41, ...), custom_call_target="tpu_custom_call" | custom-call | flops 4831838208 | bytes 35651584 | tf_op jit(solution)/shard_map/pallas_call | solution.py:329
  213.8 47.6 %collective-permute-done.2 = bf16[1,768,2048]{2,1,0:T(8,128)(2,1)} collective-permute-done((bf16[1,768,2048]{2,1,0:T(8,128)(2,1)}, bf16[1,768,2048]{2,1,0:T(8,128)(2,1)}, u32[]{:S(2)}, u32[]{:S(2)}) %collective-permute-start.2) | collective-permute-done | bytes 3145760 | tf_op jit(solution)/shard_map/ppermute | solution.py:21
  261.4 21.8 %shard_map.129 = bf16[1536,2048]{1,0:T(8,128)(2,1)} custom-call(bf16[1536,2176]{1,0:T(8,128)(2,1)} %all-gather.3.cloned.1.call-done.moe_ref, f32[1536,2048]{1,0:T(8,128)} %shard_map.128.before_ref, bf16[2048,1536]{1,0:T(8,128)(2,1)} %bitcast.15.up_ref, bf16[768,2048]{1,0:T(8,128)(2,1)} %bitcast.16.down_ref), custom_call_target="tpu_custom_call" | custom-call | flops 14495514624 | bytes 34603008 | tf_op jit(solution)/shard_map/pallas_call | solution.py:354
  283.3 85.6 %reduce-scatter.2.cloned.1.call-done = bf16[96,2048]{1,0:T(8,128)(2,1)} async-done(((bf16[1536,2048]{1,0:T(8,128)(2,1)}), bf16[96,2048]{1,0:T(8,128)(2,1)}) %reduce-scatter.2.cloned.1.call-update) | async-done | bytes 393232 | tf_op jit(solution)/shard_map/reduce_scatter | solution.py:372
  368.9 1.9 collective-permute-done.4
  372.0 3.4 collective-permute-start.5
  375.4 9.4 %collective-permute-done.5 = bf16[192,2048]{1,0:T(8,128)(2,1)S(1)} collective-permute-done((bf16[192,2048]{1,0:T(8,128)(2,1)S(1)}, bf16[192,2048]{1,0:T(8,128)(2,1)S(1)}, u32[]{:S(2)}, u32[]{:S(2)}) %collective-permute-start.5) | collective-permute-done | bytes 786464 | tf_op jit(solution)/shard_map/ppermute | solution.py:378
  384.8 1.3 fusion.10
  (52 shorter events, 11.7 us)
Async XLA Ops:
  6.5 4.9 %copy-start = (bf16[16,2048]{1,0:T(8,128)(2,1)S(1)}, bf16[16,2048]{1,0:T(8,128)(2,1)}, u32[]{:S(2)}) copy-start(bf16[16,2048]{1,0:T(8,128)(2,1)} %param.22) | copy-start | bytes 196612
  6.5 3.8 copy-start.2
  6.5 3.8 copy-start.4
  6.5 138.2 %all-gather.3.cloned.1.call-start = ((), (), s32[]{:S(2)}) async-start(), calls=%async_computation.2 | async-start | bytes 7102464 | tf_op jit(solution)/shard_map/all_gather | solution.py:294
  12.3 4.4 %collective-permute-start = (bf16[96,4224]{1,0:T(8,128)(2,1)S(1)}, bf16[96,4224]{1,0:T(8,128)(2,1)}, u32[]{:S(2)}, u32[]{:S(2)}) collective-permute-start(bf16[96,4224]{1,0:T(8,128)(2,1)S(1)} %constant_dynamic-slice_fusion), channel_id=1, source_target_pairs={{0,2},{3,1},{4,6},{7,5},{8,10},{11,9},{12,14},{15,13},{16,18},{19,... | collective-permute-start | bytes 2433032 | tf_op jit(solution)/shard_map/ppermute | solution.py:292
  15.5 3.1 copy-start.5
  15.5 3.1 copy-start.6
  17.7 178.6 %all-gather.5.cloned.1.call-start = ((), (), s32[]{:S(2)}) async-start(), calls=%async_computation.3 | async-start | bytes 6684672 | tf_op jit(solution)/shard_map/all_gather | solution.py:295
  18.7 26.6 %collective-permute-start.3 = (bf16[2,128,2048]{2,1,0:T(8,128)(2,1)S(1)}, bf16[2,128,2048]{2,1,0:T(8,128)(2,1)S(1)}, u32[]{:S(2)}, u32[]{:S(2)}) collective-permute-start(bf16[2,128,2048]{2,1,0:T(8,128)(2,1)S(1)} %pad_maximum_fusion.3), channel_id=1, source_target_pairs={{0,1},{1,0},{2,3},{3,2},{4,5},{5,4},{6,7},{7,6},{8,9},{9,8},{10,11... | collective-permute-start | bytes 3145736 | tf_op jit(solution)/shard_map/ppermute | solution.py:21
  45.6 1.4 copy-start.7
  49.0 88.2 %all-to-all-start = ((bf16[128,16,768]{0,2,1:T(8,128)(2,1)}), bf16[128,16,768]{0,2,1:T(8,128)(2,1)S(1)}, u32[]{:S(2)}, u32[]{:S(2)}) async-start(bf16[128,16,768]{0,2,1:T(8,128)(2,1)} %pad_maximum_fusion), calls=%async_computation | async-start | bytes 6291456 | tf_op jit(solution)/shard_map/all_to_all | solution.py:303
  55.7 313.2 %reduce-scatter.2.cloned.1.call-start = ((), (), s32[]{:S(2)}) async-start(), calls=%async_computation.4 | async-start | bytes 6684672 | tf_op jit(solution)/shard_map/reduce_scatter | solution.py:372
  55.8 205.6 %collective-permute-start.1 = (bf16[1,2048,1536]{2,1,0:T(8,128)(2,1)}, bf16[1,2048,1536]{2,1,0:T(8,128)(2,1)}, u32[]{:S(2)}, u32[]{:S(2)}) collective-permute-start(bf16[1,2048,1536]{2,1,0:T(8,128)(2,1)} %param.24), channel_id=1, source_target_pairs={{0,1},{1,0},{2,3},{3,2},{4,5},{5,4},{6,7},{7,6},{8,9},{9,8},{10,11... | collective-permute-start | bytes 18874376 | tf_op jit(solution)/shard_map/ppermute | solution.py:21
  56.5 204.9 %collective-permute-start.2 = (bf16[1,768,2048]{2,1,0:T(8,128)(2,1)}, bf16[1,768,2048]{2,1,0:T(8,128)(2,1)}, u32[]{:S(2)}, u32[]{:S(2)}) collective-permute-start(bf16[1,768,2048]{2,1,0:T(8,128)(2,1)} %param.25), channel_id=1, source_target_pairs={{0,1},{1,0},{2,3},{3,2},{4,5},{5,4},{6,7},{7,6},{8,9},{9,8},{10,11... | collective-permute-start | bytes 9437192 | tf_op jit(solution)/shard_map/ppermute | solution.py:21
  283.3 101.5 %copy-start.3 = (bf16[192,2048]{1,0:T(8,128)(2,1)S(1)}, bf16[192,2048]{1,0:T(8,128)(2,1)}, u32[]{:S(2)}) copy-start(bf16[192,2048]{1,0:T(8,128)(2,1)} %param.13) | copy-start | bytes 2359300
  368.9 1.9 collective-permute-start.4
  371.9 14.2 %copy-start.1 = (bf16[16,2048]{1,0:T(8,128)(2,1)S(1)}, bf16[16,2048]{1,0:T(8,128)(2,1)}, u32[]{:S(2)}) copy-start(bf16[16,2048]{1,0:T(8,128)(2,1)} %param.22) | copy-start | bytes 196612
  372.0 12.9 %collective-permute-start.5 = (bf16[192,2048]{1,0:T(8,128)(2,1)S(1)}, bf16[192,2048]{1,0:T(8,128)(2,1)S(1)}, u32[]{:S(2)}, u32[]{:S(2)}) collective-permute-start(bf16[192,2048]{1,0:T(8,128)(2,1)S(1)} %pad_maximum_fusion.4), channel_id=1, source_target_pairs={{0,1},{3,2},{4,5},{7,6},{8,9},{11,10},{12,13},{15,14},{16,17},{19,... | collective-permute-start | bytes 2359304 | tf_op jit(solution)/shard_map/ppermute | solution.py:378
Sparse Core Ops, SparseCore 0:
  17.8 110.1 all-gather.2
  130.3 65.9 all-gather.4
  283.4 85.4 reduce-scatter.1
